TPU v7x, 128 devices: a whole 4x4x4 slice. The times are simulated.
128 devices in a mesh: gx: 8 (over z, core), gy: 16 (over y, x).
Axes of the slice: x: 4, y: 4, z: 4, core: 2. Of those that a mesh axis runs over, the one named last changes fastest.
Arguments:
- fields: bfloat16 [2, 20, 256, 240, 128], P(None, None, 'gx', 'gy'), may hold values from -6 to 6
- cotangents: bfloat16 [2, 20, 256, 240, 128], P(None, None, 'gx', 'gy'), may hold values from -6 to 6
- w_point: bfloat16 [20, 20], replicated, may hold values from -1.25 to 1.25
- bias_vector: float32 [20], replicated, may hold values from -0.5 to 0.5
- spectral: float32 [2, 20, 20, 55296], P(None, None, None, ('gx', 'gy')), may hold values from -3 to 3
Outputs:
- activation: bfloat16 [20, 256, 240, 128], P(None, 'gx', 'gy')
- trained: float32 [2, 20, 20, 55296], P(None, None, None, ('gx', 'gy'))
All inputs are finite; a program needn't handle non-finite values.
Results may differ from a plain program's by a relative error of at most 0.008.
Values may be sent and summed in bfloat16 or wider, within the bound.
A program may use at most 128 MiB of HBM per device.

v0:
```python
import math

import jax
import jax.numpy as jnp
from jax import lax
from jax.sharding import PartitionSpec as P

NX = 256
NY = 240
NZ = 128
KX = 48
KY = 48
KZ = 24


learn_rate = 0.1


def angle_pair(positions, frequencies, length):
    product = positions[:, None] * frequencies[None, :] % length
    phase_angle = product.astype(jnp.float32) * (2.0 * math.pi / length)
    return (jnp.cos(phase_angle), jnp.sin(phase_angle))


def kept_waves(length, kept_count):
    wave_index = jnp.arange(kept_count, dtype=jnp.int32)
    return jnp.where(wave_index < kept_count // 2, wave_index, wave_index - kept_count + length)


def complex_table(positions, length, kept_count):
    cosine, sine_part = angle_pair(positions, kept_waves(length, kept_count), length)
    upper_rows = jnp.stack([cosine, -sine_part], axis=1)
    lower_rows = jnp.stack([sine_part, cosine], axis=1)
    return jnp.stack([upper_rows, lower_rows], axis=1)


def build_tables():
    cosine, sine_part = angle_pair(
        jnp.arange(NZ, dtype=jnp.int32), jnp.arange(KZ, dtype=jnp.int32), NZ
    )
    factor = jnp.where(jnp.arange(KZ) == 0, jnp.float32(1.0), jnp.float32(2.0))
    depth_forward = jnp.concatenate([cosine, -sine_part], axis=1).astype(jnp.bfloat16)
    depth_inverse = jnp.concatenate(
        [cosine.T * factor[:, None], -sine_part.T * factor[:, None]], axis=0
    ).astype(jnp.bfloat16)
    column_forward = complex_table(jnp.arange(NY, dtype=jnp.int32), NY, KY).astype(jnp.bfloat16)
    column_inverse = jnp.transpose(column_forward, (3, 2, 1, 0))
    natural_rows = jnp.arange(NX, dtype=jnp.int32)
    row_forward = complex_table(natural_rows, NX, KX).astype(jnp.bfloat16)
    row_inverse = jnp.transpose(complex_table(natural_rows, NX, KX), (3, 2, 1, 0))
    return (depth_forward, depth_inverse, column_forward, column_inverse, row_forward, row_inverse)


def spectrum(field_cells, tables):
    channels, slab_rows, slab_cols, depth_count = field_cells.shape
    moved_cells = lax.all_to_all(field_cells, "gy", split_axis=1, concat_axis=2, tiled=True)
    line_modes = jnp.dot(
        moved_cells.reshape(-1, depth_count), tables[0], preferred_element_type=jnp.float32
    ).astype(jnp.bfloat16)
    line_modes = line_modes.reshape(channels, moved_cells.shape[1], NY, 2 * KZ)
    line_rows = line_modes.shape[1]
    column_modes = jnp.einsum(
        "cxypk,ypqj->qcxjk",
        line_modes.reshape(channels, line_rows, NY, 2, KZ),
        tables[2],
        preferred_element_type=jnp.float32,
    ).astype(jnp.bfloat16)
    column_modes = column_modes.reshape(2, channels, line_rows, KY * KZ)
    gathered = lax.all_to_all(column_modes, ("gx", "gy"), split_axis=3, concat_axis=2, tiled=True)
    local_modes = gathered.shape[3]
    spectra = jnp.einsum("pcxm,xpqj->qcmj", gathered, tables[4], preferred_element_type=jnp.float32)
    return spectra.reshape(2, channels, local_modes * KX)


def field_from(mixed_modes, tables):
    inverse_total = 1.0 / (NX * NY * NZ)
    channels = mixed_modes.shape[1]
    local_modes = mixed_modes.shape[2] // KX
    blocks = mixed_modes.reshape(2, channels, local_modes, KX)
    rows_back = jnp.einsum(
        "pcmj,jpqx->qcxm",
        blocks,
        tables[5],
        precision=lax.Precision.HIGHEST,
        preferred_element_type=jnp.float32,
    )
    rows_back = (rows_back * inverse_total).astype(jnp.bfloat16)
    returned = lax.all_to_all(rows_back, ("gx", "gy"), split_axis=2, concat_axis=3, tiled=True)
    line_rows = returned.shape[2]
    line_modes = jnp.einsum(
        "pcxjk,jpqy->cxyqk",
        returned.reshape(2, channels, line_rows, KY, KZ),
        tables[3],
        preferred_element_type=jnp.float32,
    ).astype(jnp.bfloat16)
    line_modes = line_modes.reshape(channels, line_rows, NY, 2 * KZ)
    cell_values = jnp.dot(
        line_modes.reshape(-1, 2 * KZ), tables[1], preferred_element_type=jnp.float32
    ).astype(jnp.bfloat16)
    cell_values = cell_values.reshape(channels, line_rows, NY, NZ)
    result_cells = lax.all_to_all(cell_values, "gy", split_axis=2, concat_axis=1, tiled=True)
    return result_cells


def mix_modes(weights, spectra):
    real_in = spectra[0][:, None, :]
    imag_in = spectra[1][:, None, :]
    real_part = jnp.sum(weights[0] * real_in - weights[1] * imag_in, axis=0)
    imag_part = jnp.sum(weights[0] * imag_in + weights[1] * real_in, axis=0)
    return jnp.stack([real_part, imag_part])


def mode_grad(grad_spectra, spectra, weight_scale):
    grad_real = (grad_spectra[0] * weight_scale)[None]
    grad_imag = (grad_spectra[1] * weight_scale)[None]
    real_in = spectra[0][:, None, :]
    imag_in = spectra[1][:, None, :]
    return jnp.stack(
        [real_in * grad_real + imag_in * grad_imag, real_in * grad_imag - imag_in * grad_real]
    )


def shards(fields, cotangents, w_point, bias_vector, spectral):
    tables = build_tables()
    local_modes = spectral.shape[3] // KX
    owner_index = lax.axis_index("gx") * lax.axis_size("gy") + lax.axis_index("gy")
    mode_ids = owner_index * local_modes + jnp.arange(local_modes, dtype=jnp.int32)
    weight_scale = jnp.where(mode_ids % KZ == 0, jnp.float32(1.0), jnp.float32(2.0)) * (
        1.0 / (NX * NY * NZ)
    )
    weight_scale = jnp.repeat(weight_scale, KX)
    weights = spectral
    activation = None
    for step_index in range(fields.shape[0]):
        field_cells = fields[step_index]
        spectra = spectrum(field_cells, tables)
        branch = field_from(mix_modes(weights, spectra), tables)
        pre_gelu = jnp.einsum(
            "oi,ixyz->oxyz", w_point, field_cells, preferred_element_type=jnp.float32
        )
        pre_gelu = pre_gelu + branch.astype(jnp.float32) + bias_vector[:, None, None, None]
        output_value, pullback = jax.vjp(jax.nn.gelu, pre_gelu)
        grad_pre = pullback(cotangents[step_index].astype(jnp.float32))[0].astype(jnp.bfloat16)
        grad_spectra = spectrum(grad_pre, tables)
        weights = weights - learn_rate * mode_grad(grad_spectra, spectra, weight_scale)
        activation = output_value.astype(jnp.bfloat16)
    return (activation, weights)


def solution(mesh):
    return jax.shard_map(
        shards,
        mesh=mesh,
        in_specs=(
            P(None, None, "gx", "gy", None),
            P(None, None, "gx", "gy", None),
            P(),
            P(),
            P(None, None, None, ("gx", "gy")),
        ),
        out_specs=(P(None, "gx", "gy", None), P(None, None, None, ("gx", "gy"))),
        check_vma=False,
    )
```

profile of v0, /device:TPU:1, one launch (start us, length us, event | category | flops | bytes accessed | tf_op | source)
XLA Modules:
  0.0 469.3 jit_solution(6400394158269122286)
XLA Ops:
  0.6 6.4 %fusion.106 = (bf16[1,20,32,15,128]{4,2,3,1,0:T(8,128)(2,1)}, bf16[20,32,15,128]{3,1,2,0:T(8,128)(2,1)}, bf16[20,32,15,128]{3,1,2,0:T(8,128)(2,1)S(1)}, bf16[1,20,32,15,128]{4,2,3,1,0:T(8,128)(2,1)}) fusion(bf16[2,20,32,15,128]{4,2,3,1,0:T(8,128)(2,1)} %param.5), kind=kLoop, calls=%fused_computation.198 | loop fusion | bytes 14745600 | tf_op jit(solution)/shard_map/slice | solution.py:135
  9.5 7.8 %all-to-all-start = ((bf16[20,32,15,128]{3,2,0,1:T(8,128)(2,1)}), bf16[20,32,15,128]{3,2,0,1:T(8,128)(2,1)}, u32[]{:S(2)}, u32[]{:S(2)}) async-start(bf16[20,32,15,128]{3,2,0,1:T(8,128)(2,1)} %copy.241), calls=%async_computation | async-start | bytes 5242880 | tf_op jit(solution)/shard_map/all_to_all | solution.py:56
  19.7 36.6 %all-to-all-done = bf16[20,32,15,128]{3,2,0,1:T(8,128)(2,1)} async-done(((bf16[20,32,15,128]{3,2,0,1:T(8,128)(2,1)}), bf16[20,32,15,128]{3,2,0,1:T(8,128)(2,1)}, u32[]{:S(2)}, u32[]{:S(2)}) %all-to-all-start) | async-done | bytes 2457632 | tf_op jit(solution)/shard_map/all_to_all | solution.py:56
  70.5 9.0 %all-to-all-start.1 = ((bf16[128,2,360]{2,1,0:T(2,128)(2,1)}), bf16[128,2,360]{2,1,0:T(2,128)(2,1)S(1)}, u32[]{:S(2)}, u32[]{:S(2)}) async-start(bf16[128,2,360]{2,1,0:T(2,128)(2,1)} %reshape.507), calls=%async_computation.1 | async-start | bytes 393216 | tf_op jit(solution)/shard_map/all_to_all | solution.py:69
  79.6 10.4 %all-to-all-done.1 = bf16[128,2,360]{2,1,0:T(2,128)(2,1)S(1)} async-done(((bf16[128,2,360]{2,1,0:T(2,128)(2,1)}), bf16[128,2,360]{2,1,0:T(2,128)(2,1)S(1)}, u32[]{:S(2)}, u32[]{:S(2)}) %all-to-all-start.1) | async-done | bytes 184352 | tf_op jit(solution)/shard_map/all_to_all | solution.py:69
  102.1 4.2 all-to-all-start.2
  108.8 8.1 %all-to-all-done.2 = bf16[128,2,360]{2,1,0:T(2,128)(2,1)S(1)} async-done(((bf16[128,2,360]{2,1,0:T(2,128)(2,1)}), bf16[128,2,360]{2,1,0:T(2,128)(2,1)S(1)}, u32[]{:S(2)}, u32[]{:S(2)}) %all-to-all-start.2) | async-done | bytes 184352 | tf_op jit(solution)/shard_map/all_to_all | solution.py:88
  142.1 18.5 %all-to-all-done.6 = bf16[20,32,15,128]{3,2,0,1:T(8,128)(2,1)S(1)} async-done(((bf16[20,32,15,128]{3,2,0,1:T(8,128)(2,1)}), bf16[20,32,15,128]{3,2,0,1:T(8,128)(2,1)S(1)}, u32[]{:S(2)}, u32[]{:S(2)}) %all-to-all-start.6) | async-done | bytes 2457632 | tf_op jit(solution)/shard_map/all_to_all | solution.py:56
  160.6 4.7 all-to-all-start.3
  165.2 5.6 %fusion.105 = (bf16[1,20,32,15,128]{4,2,3,1,0:T(8,128)(2,1)}, bf16[1,20,32,15,128]{4,2,3,1,0:T(8,128)(2,1)}) fusion(bf16[2,20,32,15,128]{4,2,3,1,0:T(8,128)(2,1)} %param.6), kind=kLoop, calls=%fused_computation.197 | loop fusion | bytes 9830400 | tf_op jit(solution)/shard_map/slice | solution.py:143
  184.5 15.1 %all-to-all-done.3 = bf16[20,2,240,128]{3,1,0,2:T(2,128)(2,1)} async-done(((bf16[20,2,240,128]{3,1,0,2:T(2,128)(2,1)}), bf16[20,2,240,128]{3,1,0,2:T(2,128)(2,1)}, u32[]{:S(2)}, u32[]{:S(2)}) %all-to-all-start.3) | async-done | bytes 2457632 | tf_op jit(solution)/shard_map/all_to_all | solution.py:101
  199.6 7.1 %all-to-all-start.7 = ((bf16[128,2,360]{2,1,0:T(2,128)(2,1)}), bf16[128,2,360]{2,1,0:T(2,128)(2,1)S(1)}, u32[]{:S(2)}, u32[]{:S(2)}) async-start(bf16[128,2,360]{2,1,0:T(2,128)(2,1)} %reshape.513), calls=%async_computation.7 | async-start | bytes 393216 | tf_op jit(solution)/shard_map/all_to_all | solution.py:69
  214.5 8.8 %fusion.4 = bf16[20,32,15,128]{3,0,2,1:T(8,128)(2,1)S(1)} fusion(f32[20,16,2,15,128]{4,0,3,2,1:T(8,128)S(1)} %copy.266, bf16[1,20,32,15,128]{4,2,3,1,0:T(8,128)(2,1)S(1)} %copy-done.13, f32[20]{0:T(128)S(1)} %copy-done.42, bf16[1,20,32,15,128]{4,2,3,1,0:T(8,128)(2,1)S(1)} %copy-done.9, bf16[20,20]{1,0:T(8,128)(2,1)S(1)} %copy-done), kind=kOutput, calls=%fused_computation.18 | convolution fusion | flops 77414400 | bytes 12288880 | tf_op jit(solution)/shard_map/oi,ixyz->oxyz/dot_general | solution.py:138
  225.4 7.2 %all-to-all-start.4 = ((bf16[20,32,15,128]{3,2,0,1:T(8,128)(2,1)}), bf16[20,32,15,128]{3,2,0,1:T(8,128)(2,1)S(1)}, u32[]{:S(2)}, u32[]{:S(2)}) async-start(bf16[20,32,15,128]{3,2,0,1:T(8,128)(2,1)} %copy.267), calls=%async_computation.4 | async-start | bytes 5242880 | tf_op jit(solution)/shard_map/all_to_all | solution.py:56
  238.9 33.6 %all-to-all-done.4 = bf16[20,32,15,128]{3,2,0,1:T(8,128)(2,1)S(1)} async-done(((bf16[20,32,15,128]{3,2,0,1:T(8,128)(2,1)}), bf16[20,32,15,128]{3,2,0,1:T(8,128)(2,1)S(1)}, u32[]{:S(2)}, u32[]{:S(2)}) %all-to-all-start.4) | async-done | bytes 2457632 | tf_op jit(solution)/shard_map/all_to_all | solution.py:56
  286.9 8.3 %all-to-all-start.5 = ((bf16[128,2,360]{2,1,0:T(2,128)(2,1)}), bf16[128,2,360]{2,1,0:T(2,128)(2,1)S(1)}, u32[]{:S(2)}, u32[]{:S(2)}) async-start(bf16[128,2,360]{2,1,0:T(2,128)(2,1)} %reshape.511), calls=%async_computation.5 | async-start | bytes 393216 | tf_op jit(solution)/shard_map/all_to_all | solution.py:69
  295.5 10.1 %all-to-all-done.5 = bf16[128,2,360]{2,1,0:T(2,128)(2,1)S(1)} async-done(((bf16[128,2,360]{2,1,0:T(2,128)(2,1)}), bf16[128,2,360]{2,1,0:T(2,128)(2,1)S(1)}, u32[]{:S(2)}, u32[]{:S(2)}) %all-to-all-start.5) | async-done | bytes 184352 | tf_op jit(solution)/shard_map/all_to_all | solution.py:69
  314.6 14.9 %all_to_all.180 = bf16[128,2,360]{2,1,0:T(2,128)(2,1)S(1)} all-to-all(bf16[128,2,360]{2,1,0:T(2,128)(2,1)S(1)} %reshape.515), channel_id=1, replica_groups=mesh['gx'=8,'gy'=16] {'gx','gy'}, dimensions={0} | all-to-all | bytes 368640 | tf_op jit(solution)/shard_map/all_to_all | solution.py:88
  339.2 34.3 %all_to_all.181 = bf16[20,2,240,128]{3,1,0,2:T(2,128)(2,1)S(1)} all-to-all(bf16[20,2,240,128]{3,1,0,2:T(2,128)(2,1)S(1)} %copy.297), channel_id=1, replica_groups=mesh['gx'=8,'gy'=16] {'gy'}, dimensions={2} | all-to-all | bytes 4915200 | tf_op jit(solution)/shard_map/all_to_all | solution.py:101
  379.6 8.9 %fusion.9 = (bf16[20,32,15,128]{3,0,2,1:T(8,128)(2,1)S(1)}, bf16[20,32,15,128]{3,0,2,1:T(8,128)(2,1)}) fusion(bf16[1,20,32,15,128]{4,2,3,1,0:T(8,128)(2,1)S(1)} %copy-done.12, f32[20]{0:T(128)S(1)} %copy-done.43, f32[20,16,2,15,128]{4,0,3,2,1:T(8,128)S(1)} %copy.300, bf16[1,20,32,15,128]{4,2,3,1,0:T(8,128)(2,1)S(1)} %copy-done.8, bf16[20,20]{1,0:T(8,128)(2,1)S(1)} %copy-done), kind=kOutput, calls=%fused_computation.23 | convolution fusion | flops 79872000 | bytes 14746480 | tf_op jit(solution)/shard_map/oi,ixyz->oxyz/dot_general | solution.py:138
  389.2 36.2 %all_to_all.182 = bf16[20,32,15,128]{3,2,0,1:T(8,128)(2,1)S(1)} all-to-all(bf16[20,32,15,128]{3,2,0,1:T(8,128)(2,1)S(1)} %copy.302), channel_id=1, replica_groups=mesh['gx'=8,'gy'=16] {'gy'}, dimensions={1} | all-to-all | bytes 4915200 | tf_op jit(solution)/shard_map/all_to_all | solution.py:56
  433.8 4.8 %reshape_reshape.23 = bf16[20,2,240,2,24]{2,1,0,4,3:T(2,128)(2,1)S(1)} reshape(bf16[9600,48]{0,1:T(8,128)(2,1)} %convolution_convert_fusion.2) | data formatting | bytes 1843200 | tf_op jit(solution)/shard_map/reshape;reshape | solution.py:64
  444.4 6.1 %all-to-all-start.11 = ((bf16[128,2,360]{2,1,0:T(2,128)(2,1)}), bf16[128,2,360]{2,1,0:T(2,128)(2,1)S(1)}, u32[]{:S(2)}, u32[]{:S(2)}) async-start(bf16[128,2,360]{2,1,0:T(2,128)(2,1)} %reshape.517), calls=%async_computation.11 | async-start | bytes 393216 | tf_op jit(solution)/shard_map/all_to_all | solution.py:69
  454.2 6.9 %all-to-all-done.11 = bf16[128,2,360]{2,1,0:T(2,128)(2,1)S(1)} async-done(((bf16[128,2,360]{2,1,0:T(2,128)(2,1)}), bf16[128,2,360]{2,1,0:T(2,128)(2,1)S(1)}, u32[]{:S(2)}, u32[]{:S(2)}) %all-to-all-start.11) | async-done | bytes 184352 | tf_op jit(solution)/shard_map/all_to_all | solution.py:69
  (215 shorter events, 153.7 us)
Async XLA Ops:
  0.6 213.8 %copy-start = (bf16[20,20]{1,0:T(8,128)(2,1)S(1)}, bf16[20,20]{1,0:T(8,128)(2,1)}, u32[]{:S(2)}) copy-start(bf16[20,20]{1,0:T(8,128)(2,1)} %param.7) | copy-start | bytes 2404
  9.5 7.8 %copy-start.1 = (f32[2,20,20,432]{3,0,2,1:T(2,128)S(1)}, f32[2,20,20,432]{3,0,2,1:T(2,128)}, u32[]{:S(2)}) copy-start(f32[2,20,20,432]{3,0,2,1:T(2,128)} %param.9) | copy-start | bytes 4147204
  9.5 46.7 %all-to-all-start = ((bf16[20,32,15,128]{3,2,0,1:T(8,128)(2,1)}), bf16[20,32,15,128]{3,2,0,1:T(8,128)(2,1)}, u32[]{:S(2)}, u32[]{:S(2)}) async-start(bf16[20,32,15,128]{3,2,0,1:T(8,128)(2,1)} %copy.241), calls=%async_computation | async-start | bytes 5242880 | tf_op jit(solution)/shard_map/all_to_all | solution.py:56
  19.0 42.0 %copy-start.33 = (bf16[128,24]{0,1:T(8,128)(2,1)}, bf16[128,24]{0,1:T(8,128)(2,1)S(1)}, u32[]{:S(2)}) copy-start(bf16[128,24]{0,1:T(8,128)(2,1)S(1)} %get-tuple-element.52) | copy-start | bytes 18436
  19.0 42.0 %copy-start.35 = (bf16[128,24]{0,1:T(8,128)(2,1)}, bf16[128,24]{0,1:T(8,128)(2,1)S(1)}, u32[]{:S(2)}) copy-start(bf16[128,24]{0,1:T(8,128)(2,1)S(1)} %get-tuple-element.53) | copy-start | bytes 18436
  19.4 111.9 %copy-start.19 = (bf16[240,1,2,48]{0,3,1,2:T(8,128)(2,1)}, bf16[240,1,2,48]{0,3,1,2:T(8,128)(2,1)S(1)}, u32[]{:S(2)}) copy-start(bf16[240,1,2,48]{0,3,1,2:T(8,128)(2,1)S(1)} %get-tuple-element.38) | copy-start | bytes 138244
  19.4 111.9 %copy-start.22 = (bf16[240,1,2,48]{0,3,1,2:T(8,128)(2,1)}, bf16[240,1,2,48]{0,3,1,2:T(8,128)(2,1)S(1)}, u32[]{:S(2)}) copy-start(bf16[240,1,2,48]{0,3,1,2:T(8,128)(2,1)S(1)} %get-tuple-element.39) | copy-start | bytes 138244
  70.5 19.5 %all-to-all-start.1 = ((bf16[128,2,360]{2,1,0:T(2,128)(2,1)}), bf16[128,2,360]{2,1,0:T(2,128)(2,1)S(1)}, u32[]{:S(2)}, u32[]{:S(2)}) async-start(bf16[128,2,360]{2,1,0:T(2,128)(2,1)} %reshape.507), calls=%async_computation.1 | async-start | bytes 393216 | tf_op jit(solution)/shard_map/all_to_all | solution.py:69
  79.5 15.5 %copy-start.14 = (f32[256,1,2,48]{0,3,1,2:T(8,128)}, f32[256,1,2,48]{0,3,1,2:T(8,128)S(1)}, u32[]{:S(2)}) copy-start(f32[256,1,2,48]{0,3,1,2:T(8,128)S(1)} %get-tuple-element.36) | copy-start | bytes 294916
  79.5 15.5 %copy-start.16 = (f32[256,1,2,48]{0,3,1,2:T(8,128)}, f32[256,1,2,48]{0,3,1,2:T(8,128)S(1)}, u32[]{:S(2)}) copy-start(f32[256,1,2,48]{0,3,1,2:T(8,128)S(1)} %get-tuple-element.37) | copy-start | bytes 294916
  79.6 13.5 %copy-start.10 = (bf16[256,2,2,48,1]{0,3,4,1,2:T(8,128)(2,1)}, bf16[256,2,2,48,1]{0,3,4,1,2:T(8,128)(2,1)S(1)}, u32[]{:S(2)}) copy-start(bf16[256,2,2,48,1]{0,3,4,1,2:T(8,128)(2,1)S(1)} %fusion.62) | copy-start | bytes 294916
  94.8 11.6 %copy-start.4 = (bf16[20,32,15,128]{3,1,2,0:T(8,128)(2,1)S(1)}, bf16[20,32,15,128]{3,1,2,0:T(8,128)(2,1)}, u32[]{:S(2)}) copy-start(bf16[20,32,15,128]{3,1,2,0:T(8,128)(2,1)} %get-tuple-element.21) | copy-start | bytes 7372804
  102.1 14.8 %all-to-all-start.2 = ((bf16[128,2,360]{2,1,0:T(2,128)(2,1)}), bf16[128,2,360]{2,1,0:T(2,128)(2,1)S(1)}, u32[]{:S(2)}, u32[]{:S(2)}) async-start(bf16[128,2,360]{2,1,0:T(2,128)(2,1)} %reshape.509), calls=%async_computation.2 | async-start | bytes 393216 | tf_op jit(solution)/shard_map/all_to_all | solution.py:88
  117.0 43.6 %all-to-all-start.6 = ((bf16[20,32,15,128]{3,2,0,1:T(8,128)(2,1)}), bf16[20,32,15,128]{3,2,0,1:T(8,128)(2,1)S(1)}, u32[]{:S(2)}, u32[]{:S(2)}) async-start(bf16[20,32,15,128]{3,2,0,1:T(8,128)(2,1)} %copy.278), calls=%async_computation.6 | async-start | bytes 5242880 | tf_op jit(solution)/shard_map/all_to_all | solution.py:56
  160.6 39.0 %all-to-all-start.3 = ((bf16[20,2,240,128]{3,1,0,2:T(2,128)(2,1)}), bf16[20,2,240,128]{3,1,0,2:T(2,128)(2,1)}, u32[]{:S(2)}, u32[]{:S(2)}) async-start(bf16[20,2,240,128]{3,1,0,2:T(2,128)(2,1)} %copy.263), calls=%async_computation.3 | async-start | bytes 4915200 | tf_op jit(solution)/shard_map/all_to_all | solution.py:101
  199.6 25.8 %all-to-all-start.7 = ((bf16[128,2,360]{2,1,0:T(2,128)(2,1)}), bf16[128,2,360]{2,1,0:T(2,128)(2,1)S(1)}, u32[]{:S(2)}, u32[]{:S(2)}) async-start(bf16[128,2,360]{2,1,0:T(2,128)(2,1)} %reshape.513), calls=%async_computation.7 | async-start | bytes 393216 | tf_op jit(solution)/shard_map/all_to_all | solution.py:69
  225.4 47.0 %all-to-all-start.4 = ((bf16[20,32,15,128]{3,2,0,1:T(8,128)(2,1)}), bf16[20,32,15,128]{3,2,0,1:T(8,128)(2,1)S(1)}, u32[]{:S(2)}, u32[]{:S(2)}) async-start(bf16[20,32,15,128]{3,2,0,1:T(8,128)(2,1)} %copy.267), calls=%async_computation.4 | async-start | bytes 5242880 | tf_op jit(solution)/shard_map/all_to_all | solution.py:56
  232.6 5.1 %copy-start.11 = (bf16[256,2,2,48,1]{0,3,4,1,2:T(8,128)(2,1)S(1)}, bf16[256,2,2,48,1]{0,3,4,1,2:T(8,128)(2,1)}, u32[]{:S(2)}) copy-start(bf16[256,2,2,48,1]{0,3,4,1,2:T(8,128)(2,1)} %copy-done.10) | copy-start | bytes 294916
  232.8 76.3 %copy-start.40 = (f32[432]{0:T(512)}, f32[432]{0:T(512)S(1)}, u32[]{:S(2)}) copy-start(f32[432]{0:T(512)S(1)} %mul.616) | copy-start | bytes 5188
  281.1 14.1 %copy-start.18 = (f32[2,20,9,48]{3,1,2,0:T(8,128)S(1)}, f32[2,20,9,48]{3,1,2,0:T(8,128)}, u32[]{:S(2)}) copy-start(f32[2,20,9,48]{3,1,2,0:T(8,128)} %convolution_bitcast_fusion.7) | copy-start | bytes 207364
  286.9 18.7 %all-to-all-start.5 = ((bf16[128,2,360]{2,1,0:T(2,128)(2,1)}), bf16[128,2,360]{2,1,0:T(2,128)(2,1)S(1)}, u32[]{:S(2)}, u32[]{:S(2)}) async-start(bf16[128,2,360]{2,1,0:T(2,128)(2,1)} %reshape.511), calls=%async_computation.5 | async-start | bytes 393216 | tf_op jit(solution)/shard_map/all_to_all | solution.py:69
  295.3 14.9 %copy-start.29 = (f32[20,432]{1,0:T(8,128)}, f32[20,432]{1,0:T(8,128)S(1)}, u32[]{:S(2)}) copy-start(f32[20,432]{1,0:T(8,128)S(1)} %mul.628) | copy-start | bytes 103684
  295.5 14.8 %copy-start.31 = (f32[20,432]{1,0:T(8,128)}, f32[20,432]{1,0:T(8,128)S(1)}, u32[]{:S(2)}) copy-start(f32[20,432]{1,0:T(8,128)S(1)} %mul.631) | copy-start | bytes 103684
  444.4 16.7 %all-to-all-start.11 = ((bf16[128,2,360]{2,1,0:T(2,128)(2,1)}), bf16[128,2,360]{2,1,0:T(2,128)(2,1)S(1)}, u32[]{:S(2)}, u32[]{:S(2)}) async-start(bf16[128,2,360]{2,1,0:T(2,128)(2,1)} %reshape.517), calls=%async_computation.11 | async-start | bytes 393216 | tf_op jit(solution)/shard_map/all_to_all | solution.py:69
  (29 other events, 65.5 us)
where the time goes:
time: 477 us; the launch traced here: 469 us
  local copies, waits for them, and re-layouts  142 us (30%)
  waiting for transfers between devices  139 us (29%)
  blocking collectives  85.4 us (18%)
  starting transfers between devices  58.2 us (12%)
  matrix products  35.5 us (7%)
  other arithmetic  6.56 us (1%)
    all_to_all x3, waiting for transfers between devices, spectrum(): lax.all_to_all(field_cells, 'gy', split_axis=1, concat_axis=2, tiled=True)  88.7 us
    all_to_all x1, blocking collectives, spectrum(): lax.all_to_all(field_cells, 'gy', split_axis=1, concat_axis=2, tiled=True)  36.2 us
    unnamed x103, local copies, waits for them, and re-layouts  35.2 us
    all_to_all x1, blocking collectives, field_from(): lax.all_to_all(cell_values, 'gy', split_axis=2, concat_axis=1, tiled=True)  34.3 us
    all_to_all x4, starting transfers between devices, spectrum(): lax.all_to_all(column_modes, ('gx', 'gy'), split_axis=3, concat_axis=2, t...  30.5 us
    all_to_all x4, waiting for transfers between devices, spectrum(): lax.all_to_all(column_modes, ('gx', 'gy'), split_axis=3, concat_axis=2, t...  27.4 us
    all_to_all x3, starting transfers between devices, spectrum(): lax.all_to_all(field_cells, 'gy', split_axis=1, concat_axis=2, tiled=True)  18.8 us
    dot_general x2, matrix products, shards(): jnp.einsum('oi,ixyz->oxyz', w_point, field_cells, preferred_element_type=...  17.8 us
  transfers between devices with their start and end apart: 9, of which 8 were waited for; matrix products, arithmetic and copies ran while one was open for 16% of the time, Pallas kernels for 0%

commit v1 on v0

--- a/solution.py
+++ b/solution.py
@@ -53,11 +53,11 @@
 
 def spectrum(field_cells, tables):
     channels, slab_rows, slab_cols, depth_count = field_cells.shape
-    moved_cells = lax.all_to_all(field_cells, "gy", split_axis=1, concat_axis=2, tiled=True)
-    line_modes = jnp.dot(
-        moved_cells.reshape(-1, depth_count), tables[0], preferred_element_type=jnp.float32
+    depth_modes = jnp.dot(
+        field_cells.reshape(-1, depth_count), tables[0], preferred_element_type=jnp.float32
     ).astype(jnp.bfloat16)
-    line_modes = line_modes.reshape(channels, moved_cells.shape[1], NY, 2 * KZ)
+    depth_modes = depth_modes.reshape(channels, slab_rows, slab_cols, 2 * KZ)
+    line_modes = lax.all_to_all(depth_modes, "gy", split_axis=1, concat_axis=2, tiled=True)
     line_rows = line_modes.shape[1]
     column_modes = jnp.einsum(
         "cxypk,ypqj->qcxjk",
@@ -94,12 +94,11 @@
         preferred_element_type=jnp.float32,
     ).astype(jnp.bfloat16)
     line_modes = line_modes.reshape(channels, line_rows, NY, 2 * KZ)
+    slab_modes = lax.all_to_all(line_modes, "gy", split_axis=2, concat_axis=1, tiled=True)
     cell_values = jnp.dot(
-        line_modes.reshape(-1, 2 * KZ), tables[1], preferred_element_type=jnp.float32
+        slab_modes.reshape(-1, 2 * KZ), tables[1], preferred_element_type=jnp.float32
     ).astype(jnp.bfloat16)
-    cell_values = cell_values.reshape(channels, line_rows, NY, NZ)
-    result_cells = lax.all_to_all(cell_values, "gy", split_axis=2, concat_axis=1, tiled=True)
-    return result_cells
+    return cell_values.reshape(channels, slab_modes.shape[1], slab_modes.shape[2], NZ)
 
 
 def mix_modes(weights, spectra):

time: 477 us -> 628 us (1.32)
  local copies, waits for them, and re-layouts: 142 us -> 391 us
  waiting for transfers between devices: 139 us -> 39.3 us
  blocking collectives: 85.4 us -> 50.6 us
  other arithmetic: 6.56 us -> 25.6 us
  matrix products: 35.5 us -> 43.6 us
  starting transfers between devices: 58.2 us -> 66.3 us
    reshape x6 -> x22, local copies, waits for them, and re-layouts: 18.6 us -> 132 us  [the longest x8 70.9 us: spectrum(): line_modes.reshape(channels, line_rows, NY, 2, KZ)]
    unnamed x103 -> x92, local copies, waits for them, and re-layouts: 35.2 us -> 123 us
    all_to_all x4 -> x5, waiting for transfers between devices: 104 us -> 19.7 us  [the longest x2 10.1 us: field_from(): lax.all_to_all(line_modes, 'gy', split_axis=2, concat_axis=1, tiled=True)]
    all_to_all x2, blocking collectives: 70.4 us -> 34.9 us  [the longest x1 18.6 us: spectrum(): lax.all_to_all(depth_modes, 'gy', split_axis=1, concat_axis=2, tiled=True)]
    all_to_all x4 -> x6, local copies, waits for them, and re-layouts: 9.17 us -> 32.6 us  [the longest x4 26.4 us: spectrum(): lax.all_to_all(depth_modes, 'gy', split_axis=1, concat_axis=2, tiled=True)]
    convert_element_type x2, other arithmetic: 2.74 us -> 17.4 us  [shards(): pullback(cotangents[step_index].astype(jnp.float32))[0].astype(jnp.bfloat16)]
    convert_element_type x0 -> x4, local copies, waits for them, and re-layouts: none -> 10.2 us  [spectrum(): depth_modes = jnp.dot(field_cells.reshape(-1, depth_count), tables[0], pr...]
    all_to_all x4 -> x5, starting transfers between devices: 23.5 us -> 32.8 us  [the longest x3 21.5 us: spectrum(): lax.all_to_all(depth_modes, 'gy', split_axis=1, concat_axis=2, tiled=True)]
  transfers between devices with their start and end apart: 9 -> 9, of which waited for: 8 -> 5; matrix products, arithmetic and copies ran while one was open for 16% -> 30% of each run, Pallas kernels for 0% -> 0%
where the time goes in v1:
time: 628 us; the launch traced here: 618 us
  local copies, waits for them, and re-layouts  391 us (62%)
  starting transfers between devices  66.3 us (11%)
  blocking collectives  50.6 us (8%)
  matrix products  43.6 us (7%)
  waiting for transfers between devices  39.3 us (6%)
  other arithmetic  25.6 us (4%)
    unnamed x92, local copies, waits for them, and re-layouts  123 us
    reshape x8, local copies, waits for them, and re-layouts, spectrum(): line_modes.reshape(channels, line_rows, NY, 2, KZ)  70.9 us
    reshape x8, local copies, waits for them, and re-layouts, spectrum(): depth_modes = depth_modes.reshape(channels, slab_rows, slab_cols, 2 * KZ)  33.7 us
    all_to_all x3, starting transfers between devices, spectrum(): lax.all_to_all(column_modes, ('gx', 'gy'), split_axis=3, concat_axis=2, t...  27.9 us
    all_to_all x4, local copies, waits for them, and re-layouts, spectrum(): lax.all_to_all(depth_modes, 'gy', split_axis=1, concat_axis=2, tiled=True)  26.4 us
    all_to_all x3, starting transfers between devices, spectrum(): lax.all_to_all(depth_modes, 'gy', split_axis=1, concat_axis=2, tiled=True)  21.5 us
    all_to_all x3, waiting for transfers between devices, spectrum(): lax.all_to_all(column_modes, ('gx', 'gy'), split_axis=3, concat_axis=2, t...  19.6 us
    all_to_all x1, blocking collectives, spectrum(): lax.all_to_all(depth_modes, 'gy', split_axis=1, concat_axis=2, tiled=True)  18.6 us
  transfers between devices with their start and end apart: 9, of which 5 were waited for; matrix products, arithmetic and copies ran while one was open for 30% of the time, Pallas kernels for 0%

profile of v1, /device:TPU:1, one launch (start us, length us, event | category | flops | bytes accessed | tf_op | source)
XLA Modules:
  0.0 617.8 jit_solution(9435533611210895606)
XLA Ops:
  33.2 7.8 %all-to-all-start = ((bf16[16,2,14400]{2,1,0:T(2,128)(2,1)}), bf16[16,2,14400]{2,1,0:T(2,128)(2,1)S(1)}, u32[]{:S(2)}, u32[]{:S(2)}) async-start(bf16[16,2,14400]{2,1,0:T(2,128)(2,1)} %reshape.537), calls=%async_computation | async-start | bytes 1851392 | tf_op jit(solution)/shard_map/all_to_all | solution.py:60
  67.2 11.0 %reshape.483 = bf16[20,2,240,2,24]{4,3,1,2,0:T(2,128)(2,1)} reshape(bf16[20,2,16,15,48]{4,1,3,2,0:T(2,128)(2,1)} %bitcast.343) | data formatting | bytes 1843200 | tf_op jit(solution)/shard_map/reshape | solution.py:64
  78.2 8.4 %copy.275 = bf16[20,2,240,2,24]{2,4,3,1,0:T(8,128)(2,1)S(1)} copy(bf16[20,2,240,2,24]{4,3,1,2,0:T(2,128)(2,1)} %reshape.483) | data formatting | bytes 1843200 | tf_op jit(solution)/shard_map/reshape | solution.py:64
  97.2 8.5 %all-to-all-start.1 = ((bf16[128,2,360]{2,1,0:T(2,128)(2,1)}), bf16[128,2,360]{2,1,0:T(2,128)(2,1)S(1)}, u32[]{:S(2)}, u32[]{:S(2)}) async-start(bf16[128,2,360]{2,1,0:T(2,128)(2,1)} %reshape.539), calls=%async_computation.1 | async-start | bytes 393216 | tf_op jit(solution)/shard_map/all_to_all | solution.py:69
  105.8 10.5 %all-to-all-done.1 = bf16[128,2,360]{2,1,0:T(2,128)(2,1)S(1)} async-done(((bf16[128,2,360]{2,1,0:T(2,128)(2,1)}), bf16[128,2,360]{2,1,0:T(2,128)(2,1)S(1)}, u32[]{:S(2)}, u32[]{:S(2)}) %all-to-all-start.1) | async-done | bytes 184352 | tf_op jit(solution)/shard_map/all_to_all | solution.py:69
  180.1 7.6 %reshape.543 = bf16[16,2,14400]{2,1,0:T(2,128)(2,1)} reshape(bf16[240,20,2,48]{3,2,1,0:T(2,128)(2,1)} %bitcast.347) | data formatting | bytes 1843200
  208.1 7.0 %copy.452 = bf16[20,16,2,15,48]{4,2,3,1,0:T(2,128)(2,1)} copy(bf16[20,16,2,15,48]{4,3,0,2,1:T(8,128)(2,1)} %bitcast.338) | data formatting | bytes 1843200 | tf_op jit(solution)/shard_map/all_to_all | solution.py:60
  215.1 11.0 %reshape.493 = bf16[20,2,240,2,24]{4,3,1,2,0:T(2,128)(2,1)} reshape(bf16[20,2,16,15,48]{4,1,3,2,0:T(2,128)(2,1)} %bitcast.344) | data formatting | bytes 1843200 | tf_op jit(solution)/shard_map/reshape | solution.py:64
  226.1 8.4 %copy.316 = bf16[20,2,240,2,24]{2,4,3,1,0:T(8,128)(2,1)S(1)} copy(bf16[20,2,240,2,24]{4,3,1,2,0:T(2,128)(2,1)} %reshape.493) | data formatting | bytes 1843200 | tf_op jit(solution)/shard_map/reshape | solution.py:64
  245.6 11.9 %all-to-all-start.7 = ((bf16[128,2,360]{2,1,0:T(2,128)(2,1)}), bf16[128,2,360]{2,1,0:T(2,128)(2,1)}, u32[]{:S(2)}, u32[]{:S(2)}) async-start(bf16[128,2,360]{2,1,0:T(2,128)(2,1)} %reshape.551), calls=%async_computation.7 | async-start | bytes 393216 | tf_op jit(solution)/shard_map/all_to_all | solution.py:69
  257.6 8.0 %reshape.544 = bf16[240,20,2,48]{3,2,1,0:T(2,128)(2,1)} reshape(bf16[16,2,14400]{2,1,0:T(2,128)(2,1)} %all-to-all-done.3) | data formatting | bytes 1843200
  285.4 8.1 %fusion.6 = bf16[20,32,15,128]{3,1,2,0:T(8,128)(2,1)S(1)} fusion(f32[20,32,15,128]{3,2,1,0:T(8,128)} %reshape.503, f32[20,32,15,128]{3,0,2,1:T(8,128)} %fusion.26, f32[20]{0:T(128)S(1)} %copy-done.31, bf16[2,20,32,15,128]{4,2,3,1,0:T(8,128)(2,1)} %param.6), kind=kLoop, calls=%fused_computation.20 | loop fusion | flops 28262400 | bytes 14745680 | tf_op jit(solution)/shard_map/convert_element_type | solution.py:142
  354.7 11.0 %reshape.490 = bf16[20,2,240,2,24]{4,3,1,2,0:T(2,128)(2,1)} reshape(bf16[20,2,16,15,48]{4,1,3,2,0:T(2,128)(2,1)} %bitcast.345) | data formatting | bytes 1843200 | tf_op jit(solution)/shard_map/reshape | solution.py:64
  365.6 8.4 %copy.303 = bf16[20,2,240,2,24]{2,4,3,1,0:T(8,128)(2,1)S(1)} copy(bf16[20,2,240,2,24]{4,3,1,2,0:T(2,128)(2,1)} %reshape.490) | data formatting | bytes 1843200 | tf_op jit(solution)/shard_map/reshape | solution.py:64
  385.6 7.4 %all-to-all-start.5 = ((bf16[128,2,360]{2,1,0:T(2,128)(2,1)}), bf16[128,2,360]{2,1,0:T(2,128)(2,1)S(1)}, u32[]{:S(2)}, u32[]{:S(2)}) async-start(bf16[128,2,360]{2,1,0:T(2,128)(2,1)} %reshape.547), calls=%async_computation.5 | async-start | bytes 393216 | tf_op jit(solution)/shard_map/all_to_all | solution.py:69
  394.5 9.1 %all-to-all-done.5 = bf16[128,2,360]{2,1,0:T(2,128)(2,1)S(1)} async-done(((bf16[128,2,360]{2,1,0:T(2,128)(2,1)}), bf16[128,2,360]{2,1,0:T(2,128)(2,1)S(1)}, u32[]{:S(2)}, u32[]{:S(2)}) %all-to-all-start.5) | async-done | bytes 184352 | tf_op jit(solution)/shard_map/all_to_all | solution.py:69
  428.2 15.7 %all_to_all.192 = bf16[128,2,360]{2,1,0:T(2,128)(2,1)} all-to-all(bf16[128,2,360]{2,1,0:T(2,128)(2,1)} %reshape.553), channel_id=1, replica_groups=mesh['gx'=8,'gy'=16] {'gx','gy'}, dimensions={0} | all-to-all | bytes 368640 | tf_op jit(solution)/shard_map/all_to_all | solution.py:88
  464.7 7.6 %reshape.555 = bf16[16,2,14400]{2,1,0:T(2,128)(2,1)} reshape(bf16[240,20,2,48]{3,2,1,0:T(2,128)(2,1)} %bitcast.349) | data formatting | bytes 1843200
  481.7 10.1 %all-to-all-done.9 = bf16[16,2,14400]{2,1,0:T(2,128)(2,1)} async-done(((bf16[16,2,14400]{2,1,0:T(2,128)(2,1)}), bf16[16,2,14400]{2,1,0:T(2,128)(2,1)}, u32[]{:S(2)}, u32[]{:S(2)}) %all-to-all-start.9) | async-done | bytes 921632 | tf_op jit(solution)/shard_map/all_to_all | solution.py:97
  491.8 7.3 %reshape.556 = bf16[240,20,2,48]{3,2,1,0:T(2,128)(2,1)S(1)} reshape(bf16[16,2,14400]{2,1,0:T(2,128)(2,1)} %all-to-all-done.9) | data formatting | bytes 1843200
  514.9 9.3 %fusion.11 = (bf16[20,32,15,128]{3,1,2,0:T(8,128)(2,1)S(1)}, bf16[20,32,15,128]{3,1,2,0:T(8,128)(2,1)}) fusion(bf16[2,20,32,15,128]{4,2,3,1,0:T(8,128)(2,1)} %param.6, f32[20]{0:T(128)} %param.8, f32[20,32,15,128]{3,2,1,0:T(8,128)} %reshape.504, f32[20,32,15,128]{3,0,2,1:T(8,128)} %fusion.27), kind=kLoop, calls=%fused_computation.25 | loop fusion | flops 30720000 | bytes 17203280 | tf_op jit(solution)/shard_map/convert_element_type | solution.py:142
  547.5 18.6 %all_to_all.193 = bf16[16,2,14400]{2,1,0:T(2,128)(2,1)S(1)} all-to-all(bf16[16,2,14400]{2,1,0:T(2,128)(2,1)S(1)} %reshape.557), channel_id=1, replica_groups=mesh['gx'=8,'gy'=16] {'gy'}, dimensions={0} | all-to-all | bytes 1843200 | tf_op jit(solution)/shard_map/all_to_all | solution.py:60
  580.5 8.4 %copy.342 = bf16[20,2,240,2,24]{2,4,3,1,0:T(8,128)(2,1)S(1)} copy(bf16[20,2,240,2,24]{4,3,1,2,0:T(2,128)(2,1)} %reshape.500) | data formatting | bytes 1843200 | tf_op jit(solution)/shard_map/reshape | solution.py:64
  593.2 16.3 %all_to_all.194 = bf16[128,2,360]{2,1,0:T(2,128)(2,1)S(1)} all-to-all(bf16[128,2,360]{2,1,0:T(2,128)(2,1)S(1)} %reshape.559), channel_id=1, replica_groups=mesh['gx'=8,'gy'=16] {'gx','gy'}, dimensions={0} | all-to-all | bytes 368640 | tf_op jit(solution)/shard_map/all_to_all | solution.py:69
  (219 shorter events, 378.6 us)
Async XLA Ops:
  0.6 194.6 %copy-start = (bf16[20,20]{1,0:T(8,128)(2,1)S(1)}, bf16[20,20]{1,0:T(8,128)(2,1)}, u32[]{:S(2)}) copy-start(bf16[20,20]{1,0:T(8,128)(2,1)} %param.7) | copy-start | bytes 2404
  0.7 12.4 %copy-start.24 = (bf16[128,24]{0,1:T(8,128)(2,1)}, bf16[128,24]{0,1:T(8,128)(2,1)S(1)}, u32[]{:S(2)}) copy-start(bf16[128,24]{0,1:T(8,128)(2,1)S(1)} %get-tuple-element.49) | copy-start | bytes 18436
  33.2 22.4 %all-to-all-start = ((bf16[16,2,14400]{2,1,0:T(2,128)(2,1)}), bf16[16,2,14400]{2,1,0:T(2,128)(2,1)S(1)}, u32[]{:S(2)}, u32[]{:S(2)}) async-start(bf16[16,2,14400]{2,1,0:T(2,128)(2,1)} %reshape.537), calls=%async_computation | async-start | bytes 1851392 | tf_op jit(solution)/shard_map/all_to_all | solution.py:60
  51.9 34.7 %copy-start.6 = (bf16[240,1,2,48]{0,3,1,2:T(8,128)(2,1)}, bf16[240,1,2,48]{0,3,1,2:T(8,128)(2,1)S(1)}, u32[]{:S(2)}) copy-start(bf16[240,1,2,48]{0,3,1,2:T(8,128)(2,1)S(1)} %get-tuple-element.34) | copy-start | bytes 138244
  52.0 34.7 %copy-start.9 = (bf16[240,1,2,48]{0,3,1,2:T(8,128)(2,1)}, bf16[240,1,2,48]{0,3,1,2:T(8,128)(2,1)S(1)}, u32[]{:S(2)}) copy-start(bf16[240,1,2,48]{0,3,1,2:T(8,128)(2,1)S(1)} %get-tuple-element.35) | copy-start | bytes 138244
  87.9 17.8 %copy-start.21 = (f32[256,1,48]{0,2,1:T(8,128)S(1)}, f32[256,1,48]{0,2,1:T(8,128)}, u32[]{:S(2)}) copy-start(f32[256,1,48]{0,2,1:T(8,128)} %get-tuple-element.45) | copy-start | bytes 147460
  87.9 17.8 %copy-start.22 = (f32[256,1,48]{0,2,1:T(8,128)S(1)}, f32[256,1,48]{0,2,1:T(8,128)}, u32[]{:S(2)}) copy-start(f32[256,1,48]{0,2,1:T(8,128)} %get-tuple-element.46) | copy-start | bytes 147460
  87.9 17.8 %copy-start.23 = (f32[256,1,48]{0,2,1:T(8,128)S(1)}, f32[256,1,48]{0,2,1:T(8,128)}, u32[]{:S(2)}) copy-start(f32[256,1,48]{0,2,1:T(8,128)} %get-tuple-element.47) | copy-start | bytes 147460
  97.2 19.1 %all-to-all-start.1 = ((bf16[128,2,360]{2,1,0:T(2,128)(2,1)}), bf16[128,2,360]{2,1,0:T(2,128)(2,1)S(1)}, u32[]{:S(2)}, u32[]{:S(2)}) async-start(bf16[128,2,360]{2,1,0:T(2,128)(2,1)} %reshape.539), calls=%async_computation.1 | async-start | bytes 393216 | tf_op jit(solution)/shard_map/all_to_all | solution.py:69
  105.8 18.5 %copy-start.12 = (f32[256,1,2,48]{0,3,1,2:T(8,128)}, f32[256,1,2,48]{0,3,1,2:T(8,128)S(1)}, u32[]{:S(2)}) copy-start(f32[256,1,2,48]{0,3,1,2:T(8,128)S(1)} %get-tuple-element.32) | copy-start | bytes 294916
  105.8 18.5 %copy-start.13 = (f32[256,1,2,48]{0,3,1,2:T(8,128)}, f32[256,1,2,48]{0,3,1,2:T(8,128)S(1)}, u32[]{:S(2)}) copy-start(f32[256,1,2,48]{0,3,1,2:T(8,128)S(1)} %get-tuple-element.33) | copy-start | bytes 294916
  123.9 13.0 %copy-start.25 = (bf16[128,24]{0,1:T(8,128)(2,1)S(1)}, bf16[128,24]{0,1:T(8,128)(2,1)}, u32[]{:S(2)}) copy-start(bf16[128,24]{0,1:T(8,128)(2,1)} %copy-done.24) | copy-start | bytes 18436
  131.2 25.7 %all-to-all-start.2 = ((bf16[128,2,360]{2,1,0:T(2,128)(2,1)}), bf16[128,2,360]{2,1,0:T(2,128)(2,1)}, u32[]{:S(2)}, u32[]{:S(2)}) async-start(bf16[128,2,360]{2,1,0:T(2,128)(2,1)} %reshape.541), calls=%async_computation.2 | async-start | bytes 393216 | tf_op jit(solution)/shard_map/all_to_all | solution.py:88
  157.0 30.7 %all-to-all-start.6 = ((bf16[16,2,14400]{2,1,0:T(2,128)(2,1)}), bf16[16,2,14400]{2,1,0:T(2,128)(2,1)}, u32[]{:S(2)}, u32[]{:S(2)}) async-start(bf16[16,2,14400]{2,1,0:T(2,128)(2,1)} %reshape.549), calls=%async_computation.6 | async-start | bytes 1851392 | tf_op jit(solution)/shard_map/all_to_all | solution.py:60
  180.1 14.4 %copy-start.32 = (f32[24]{0:T(128)S(1)}, f32[24]{0:T(128)}, u32[]{:S(2)}) copy-start(f32[24]{0:T(128)} %compare_select_fusion.3) | copy-start | bytes 292
  187.7 57.9 %all-to-all-start.3 = ((bf16[16,2,14400]{2,1,0:T(2,128)(2,1)}), bf16[16,2,14400]{2,1,0:T(2,128)(2,1)}, u32[]{:S(2)}, u32[]{:S(2)}) async-start(bf16[16,2,14400]{2,1,0:T(2,128)(2,1)} %reshape.543), calls=%async_computation.3 | async-start | bytes 1851392 | tf_op jit(solution)/shard_map/all_to_all | solution.py:97
  245.6 75.5 %all-to-all-start.7 = ((bf16[128,2,360]{2,1,0:T(2,128)(2,1)}), bf16[128,2,360]{2,1,0:T(2,128)(2,1)}, u32[]{:S(2)}, u32[]{:S(2)}) async-start(bf16[128,2,360]{2,1,0:T(2,128)(2,1)} %reshape.551), calls=%async_computation.7 | async-start | bytes 393216 | tf_op jit(solution)/shard_map/all_to_all | solution.py:69
  279.2 6.2 copy-start.31
  321.1 21.9 %all-to-all-start.4 = ((bf16[16,2,14400]{2,1,0:T(2,128)(2,1)}), bf16[16,2,14400]{2,1,0:T(2,128)(2,1)S(1)}, u32[]{:S(2)}, u32[]{:S(2)}) async-start(bf16[16,2,14400]{2,1,0:T(2,128)(2,1)} %reshape.545), calls=%async_computation.4 | async-start | bytes 1851392 | tf_op jit(solution)/shard_map/all_to_all | solution.py:60
  376.2 16.9 %copy-start.14 = (f32[2,20,9,48]{3,1,2,0:T(8,128)S(1)}, f32[2,20,9,48]{3,1,2,0:T(8,128)}, u32[]{:S(2)}) copy-start(f32[2,20,9,48]{3,1,2,0:T(8,128)} %convolution_bitcast_fusion.7) | copy-start | bytes 207364
  385.6 18.0 %all-to-all-start.5 = ((bf16[128,2,360]{2,1,0:T(2,128)(2,1)}), bf16[128,2,360]{2,1,0:T(2,128)(2,1)S(1)}, u32[]{:S(2)}, u32[]{:S(2)}) async-start(bf16[128,2,360]{2,1,0:T(2,128)(2,1)} %reshape.547), calls=%async_computation.5 | async-start | bytes 393216 | tf_op jit(solution)/shard_map/all_to_all | solution.py:69
  472.3 19.5 %all-to-all-start.9 = ((bf16[16,2,14400]{2,1,0:T(2,128)(2,1)}), bf16[16,2,14400]{2,1,0:T(2,128)(2,1)}, u32[]{:S(2)}, u32[]{:S(2)}) async-start(bf16[16,2,14400]{2,1,0:T(2,128)(2,1)} %reshape.555), calls=%async_computation.9 | async-start | bytes 1851392 | tf_op jit(solution)/shard_map/all_to_all | solution.py:97
  580.5 8.5 %copy-start.8 = (bf16[240,1,2,48]{0,3,1,2:T(8,128)(2,1)S(1)}, bf16[240,1,2,48]{0,3,1,2:T(8,128)(2,1)}, u32[]{:S(2)}) copy-start(bf16[240,1,2,48]{0,3,1,2:T(8,128)(2,1)} %copy-done.6) | copy-start | bytes 138244
  580.5 8.5 %copy-start.11 = (bf16[240,1,2,48]{0,3,1,2:T(8,128)(2,1)S(1)}, bf16[240,1,2,48]{0,3,1,2:T(8,128)(2,1)}, u32[]{:S(2)}) copy-start(bf16[240,1,2,48]{0,3,1,2:T(8,128)(2,1)} %copy-done.9) | copy-start | bytes 138244
  (18 other events, 48.4 us)

commit v2 on v1

v2 whole, which is shorter than its diff:
```python
import functools
import math

import jax
import jax.numpy as jnp
import ml_dtypes
import numpy as np
from jax import lax
from jax.experimental import pallas as pl
from jax.experimental.pallas import tpu as pltpu
from jax.sharding import PartitionSpec as P

C = 20
NX, NY, NZ = 256, 240, 128
KX, KY, KZ = 48, 48, 24
GX, GY = 8, 16
LEARN_RATE = 0.1
INVERSE_TOTAL = 1.0 / (NX * NY * NZ)
BF = jnp.bfloat16
F32 = jnp.float32
MESH = pl.DeviceIdType.MESH
GELU_K = math.sqrt(2.0 / math.pi)
GELU_C = 0.044715


def waves(length, kept):
    index = np.arange(kept)
    return np.where(index < kept // 2, index, index - kept + length)


def angle_tables(length, freqs):
    product = (np.arange(length)[:, None] * freqs[None, :]) % length
    angle = product.astype(np.float32) * np.float32(2.0 * math.pi / length)
    return np.cos(angle), np.sin(angle)


def rounded(table):
    return table.astype(ml_dtypes.bfloat16)


def make_tables():
    cos_z, sin_z = angle_tables(NZ, np.arange(KZ))
    both = np.stack([cos_z, -sin_z]).transpose(0, 2, 1)
    both = both.reshape(2, 8, 3, NZ).transpose(1, 0, 2, 3)
    deep0 = np.einsum("gpkz,nm->gpnkmz", both, np.eye(8, dtype=np.float32)).reshape(384, 1024)
    deep1 = np.zeros((8, 2, 16, 4, NZ), np.float32)
    deep1[:, :, :12] = np.einsum("gpkz,nm->gpnkmz", both, np.eye(4, dtype=np.float32)).reshape(
        8, 2, 12, 4, NZ
    )
    deep1 = deep1.reshape(256, 512)
    factor = np.where(np.arange(KZ) == 0, 1.0, 2.0).astype(np.float32)
    back = np.stack([cos_z * factor, -sin_z * factor]).transpose(0, 2, 1)
    back = back.reshape(2, 8, 3, NZ).transpose(1, 0, 2, 3)
    rise0 = np.einsum("gpkz,nm->gpnkmz", back, np.eye(16, dtype=np.float32))
    rise0 = rise0.reshape(768, 8, 256).transpose(1, 0, 2)
    rise1 = np.zeros((8, 2, 16, 4, NZ), np.float32)
    rise1[:, :, :12] = np.einsum("gpkz,nm->gpnkmz", back, np.eye(4, dtype=np.float32)).reshape(
        8, 2, 12, 4, NZ
    )
    rise1 = rise1.reshape(256, 2, 256).transpose(1, 0, 2)
    cos_y, sin_y = angle_tables(NY, waves(NY, KY))
    padded = np.zeros((2, GY, 16, KY), np.float32)
    padded[:, :, :15] = np.stack([cos_y, sin_y]).reshape(2, GY, 15, KY)
    eye8 = np.eye(8, dtype=np.float32)
    column = np.einsum("asyk,xw->akxswy", padded, eye8)
    column = column.reshape(2, 2, 24 * 8, 2048).transpose(1, 0, 2, 3).reshape(2, 384, 2048)
    signed = np.stack([padded[0], -padded[1]])
    column_back = np.einsum("asyk,wx->kawsxy", signed, eye8)
    column_back = column_back.reshape(768, 8, 256).transpose(1, 0, 2)
    cos_x, sin_x = angle_tables(NX, waves(NX, KX))
    shape = (GX, 2, 2, 8, KX)
    cos_x = cos_x.reshape(shape).transpose(1, 0, 2, 3, 4)
    sin_x = sin_x.reshape(shape).transpose(1, 0, 2, 3, 4)
    row = np.zeros((2, GX, 2, 8, 2, 2, 64), np.float32)
    row_back = np.zeros_like(row)
    for xb in range(2):
        c, s = cos_x[:, :, xb], sin_x[:, :, xb]
        row[:, :, 0, :, xb, 0, :KX] = c
        row[:, :, 1, :, xb, 0, :KX] = s
        row[:, :, 0, :, xb, 1, :KX] = -s
        row[:, :, 1, :, xb, 1, :KX] = c
        row_back[:, :, 0, :, xb, 0, :KX] = c
        row_back[:, :, 0, :, xb, 1, :KX] = -s
        row_back[:, :, 1, :, xb, 0, :KX] = s
        row_back[:, :, 1, :, xb, 1, :KX] = c
    row = row.reshape(256, 256)
    row_back = row_back.reshape(256, 256)
    row_high = rounded(row_back)
    row_low = rounded(row_back - row_high.astype(np.float32))
    return (
        rounded(deep0),
        rounded(deep1),
        rounded(column),
        rounded(row),
        np.stack([row_high, row_low]),
        rounded(column_back),
        rounded(rise0),
        rounded(rise1),
    )


def dot_nt(a, b):
    return lax.dot_general(a, b, (((1,), (1,)), ((), ())), preferred_element_type=F32)


def dot_nn(a, b):
    return lax.dot_general(a, b, (((1,), (0,)), ((), ())), preferred_element_type=F32)


def kernel(
    fields_hbm, cots_hbm, w_ref, bias_ref, spectral_hbm,
    deep0_hbm, deep1_hbm, column_hbm, row_hbm, row_back_hbm, column_back_hbm, rise0_hbm, rise1_hbm,
    act_hbm, trained_hbm,
    fields, cots, cells, weights, act,
    deep0, deep1, column, row, row_back, column_back, rise0, rise1,
    send_a, recv_a, send_b, recv_b, back_b, got_b, back_a, got_a,
    xs, spectra, xi, turned, lifted, branch, kron,
    load_sems, out_sems,
    a_send, a_recv, b_send, b_recv, bb_send, bb_recv, ba_send, ba_recv,
):
    gx = lax.axis_index("gx")
    gy = lax.axis_index("gy")
    me = gx * GY + gy
    my_half = gy // 8
    my_group = gy % 8

    loads = [
        (fields_hbm.at[0], fields.at[0]),
        (deep0_hbm, deep0),
        (deep1_hbm, deep1),
        (column_hbm, column),
        (fields_hbm.at[1], fields.at[1]),
        (row_hbm, row),
        (spectral_hbm, weights),
        (row_back_hbm, row_back),
        (column_back_hbm, column_back),
        (rise0_hbm, rise0),
        (rise1_hbm, rise1),
        (cots_hbm, cots),
    ]
    copies = [
        pltpu.make_async_copy(src, dst, load_sems.at[n]) for n, (src, dst) in enumerate(loads)
    ]
    for copy in copies:
        copy.start()

    barrier = pltpu.get_barrier_semaphore()

    def greet(d, _):
        other = lax.rem(me + d, GX * GY)
        pl.semaphore_signal(
            barrier, inc=1, device_id=(other // GY, lax.rem(other, GY)), device_id_type=MESH
        )
        return 0

    lax.fori_loop(1, GX * GY, greet, 0)

    wide = lax.broadcasted_iota(jnp.int32, (C * 16, C), 0) // 16
    spread = (wide == lax.broadcasted_iota(jnp.int32, (C * 16, C), 1)).astype(BF)
    grown = dot_nt(dot_nn(spread, w_ref[...]).astype(BF), spread)
    same = lax.rem(lax.broadcasted_iota(jnp.int32, (C * 16, C * 16), 0), 16) == lax.rem(
        lax.broadcasted_iota(jnp.int32, (C * 16, C * 16), 1), 16
    )
    kron[...] = jnp.where(same, grown, 0.0).astype(BF)
    xi[...] = jnp.zeros_like(xi)

    def pad_cells(step):
        cells[step] = jnp.zeros((C, 32, 16, 128), BF)

        def one(c, _):
            cells[step, c, :, 0:15, :] = fields[step, c]
            return 0

        lax.fori_loop(0, C, one, 0)

    def deep_half(f, step, xh):
        for xb in range(2):
            rows = pl.ds((xh * 2 + xb) * 8, 8)

            def block(c):
                return cells[step, c, rows].reshape(128, 128)

            o0 = dot_nt(deep0[...], jnp.concatenate([block(c) for c in range(8)], axis=1))
            o1 = dot_nt(deep0[...], jnp.concatenate([block(c) for c in range(8, 16)], axis=1))
            o2 = dot_nt(deep1[...], jnp.concatenate([block(c) for c in range(16, 20)], axis=1))
            for group in range(8):
                for part in range(2):
                    a = group * 48 + part * 24
                    b = group * 32 + part * 16
                    send_a[f, xh * 8 + group, part, xb] = jnp.concatenate(
                        [o0[a : a + 24], o1[a : a + 24], o2[b : b + 16]], axis=0
                    ).astype(BF)

    def a_copy(f, target):
        return pltpu.make_async_remote_copy(
            src_ref=send_a.at[f, target],
            dst_ref=recv_a.at[f, gy],
            send_sem=a_send.at[f],
            recv_sem=a_recv.at[f],
            device_id=(gx, target),
            device_id_type=MESH,
        )

    def send_a_half(f, xh):
        def one(k, _):
            target = xh * 8 + lax.rem(my_group + 1 + k, 8)

            @pl.when(target == gy)
            def _():
                pltpu.make_async_copy(send_a.at[f, target], recv_a.at[f, gy], a_recv.at[f]).start()

            @pl.when(target != gy)
            def _():
                a_copy(f, target).start()

            return 0

        lax.fori_loop(0, 8, one, 0)

    def wait_all(ref, sem):
        pltpu.make_async_copy(ref, ref, sem).wait()

    def b_target(ky):
        group = lax.rem(ky, 6) * 8 + my_group
        return ky // 6, group // 3, lax.rem(group, 3)

    def b_copy(f, ky):
        other_x, other_y, slot = b_target(ky)
        return pltpu.make_async_remote_copy(
            src_ref=send_b.at[f, ky],
            dst_ref=recv_b.at[f, slot, my_half, gx],
            send_sem=b_send.at[f],
            recv_sem=b_recv.at[f],
            device_id=(other_x, other_y),
            device_id_type=MESH,
        )

    def columns(f):
        data = jnp.concatenate(
            [recv_a[f, s].reshape(256, 128) for s in range(GY)], axis=1
        )
        for part in range(2):
            out = dot_nt(column[part], data)
            real = out[:192, :128] + out[192:, 128:]
            imag = out[:192, 128:] - out[192:, :128]
            send_b[f, pl.ds(part * 24, 24)] = jnp.concatenate(
                [real.reshape(24, 8, 128), imag.reshape(24, 8, 128)], axis=1
            ).astype(BF)

            def one(k, _):
                ky = part * 24 + lax.rem(gx * 6 + gy + k, 24)
                other_x, other_y, slot = b_target(ky)
                mine = jnp.logical_and(other_x == gx, other_y == gy)

                @pl.when(mine)
                def _():
                    pltpu.make_async_copy(
                        send_b.at[f, ky], recv_b.at[f, slot, my_half, gx], b_recv.at[f]
                    ).start()

                @pl.when(jnp.logical_not(mine))
                def _():
                    b_copy(f, ky).start()

                return 0

            lax.fori_loop(0, 24, one, 0)

    def rows_forward(f):
        pieces = []
        for slot in range(3):
            data = recv_b[f, slot].reshape(256, 128)
            out = dot_nn(data.T, row[...])
            xs[slot] = out[0:64, 0:128] + out[64:128, 128:256]
            for kz in range(3):
                pieces.append(xs[slot, pl.ds(kz, C, stride=3), :])
        spectra[f, 0] = jnp.concatenate([piece[:, 0:48] for piece in pieces], axis=1)
        spectra[f, 1] = jnp.concatenate([piece[:, 64:112] for piece in pieces], axis=1)

    pair = lax.broadcasted_iota(jnp.int32, (1, 432), 1) // KX + me * 9
    scale = jnp.where(lax.rem(pair, KZ) == 0, 1.0, 2.0).astype(F32) * INVERSE_TOTAL

    def mix(f, update):
        if update is not None:
            field_f, grad_f = update
            grad_re = spectra[grad_f, 0] * scale * LEARN_RATE
            grad_im = spectra[grad_f, 1] * scale * LEARN_RATE

        def one(i, carry):
            w_re, w_im = weights[0, i], weights[1, i]
            if update is not None:
                in_re = spectra[field_f, 0, pl.ds(i, 1), :]
                in_im = spectra[field_f, 1, pl.ds(i, 1), :]
                w_re = w_re - (in_re * grad_re + in_im * grad_im)
                w_im = w_im - (in_re * grad_im - in_im * grad_re)
                weights[0, i] = w_re
                weights[1, i] = w_im
            if f is None:
                return carry
            re, im = carry
            s_re = spectra[f, 0, pl.ds(i, 1), :]
            s_im = spectra[f, 1, pl.ds(i, 1), :]
            return re + (w_re * s_re - w_im * s_im), im + (w_re * s_im + w_im * s_re)

        zero = jnp.zeros((C, 432), F32)
        return lax.fori_loop(0, C, one, (zero, zero))

    def bb_copy(step, slot, n):
        group = gy * 3 + slot
        return pltpu.make_async_remote_copy(
            src_ref=back_b.at[step, slot, n],
            dst_ref=got_b.at[step, gx * 6 + group // 8],
            send_sem=bb_send.at[step],
            recv_sem=bb_recv.at[step],
            device_id=(lax.rem(n, 8), (n // 8) * 8 + lax.rem(group, 8)),
            device_id_type=MESH,
        )

    def rows_inverse(step, mixed):
        re, im = mixed
        gap = jnp.zeros((C, 16), F32)
        for slot in range(3):
            for kz in range(3):
                a = (slot * 3 + kz) * 48
                xi[slot, pl.ds(kz, C, stride=3), :] = jnp.concatenate(
                    [re[:, a : a + 48], gap, im[:, a : a + 48], gap], axis=1
                )
            value = xi[slot]
            high = value.astype(BF)
            low = (value - high.astype(F32)).astype(BF)
            none = jnp.zeros((64, 128), BF)

            def both(v):
                return jnp.concatenate(
                    [jnp.concatenate([v, none], axis=1), jnp.concatenate([none, v], axis=1)],
                    axis=0,
                )

            high, low = both(high), both(low)
            out = dot_nt(row_back[0], high) + (dot_nt(row_back[0], low) + dot_nt(row_back[1], high))
            back_b[step, slot] = (out * INVERSE_TOTAL).astype(BF).reshape(16, 16, 128)
            group = gy * 3 + slot

            def one(k, _):
                n = lax.rem(gx + gy + k, 16)
                mine = jnp.logical_and(
                    lax.rem(n, 8) == gx, (n // 8) * 8 + lax.rem(group, 8) == gy
                )

                @pl.when(mine)
                def _():
                    pltpu.make_async_copy(
                        back_b.at[step, slot, n],
                        got_b.at[step, gx * 6 + group // 8],
                        bb_recv.at[step],
                    ).start()

                @pl.when(jnp.logical_not(mine))
                def _():
                    bb_copy(step, slot, n).start()

                return 0

            lax.fori_loop(0, 16, one, 0)

    def ba_copy(step, target):
        return pltpu.make_async_remote_copy(
            src_ref=back_a.at[step, target],
            dst_ref=got_a.at[step, gy],
            send_sem=ba_send.at[step],
            recv_sem=ba_recv.at[step, my_half],
            device_id=(gx, target),
            device_id_type=MESH,
        )

    def columns_inverse(step):
        data = got_b[step].astype(F32)
        swapped = jnp.concatenate([data[:, 8:16], -data[:, 0:8]], axis=1)
        turned[0:128, :] = data.reshape(768, 128).astype(BF).T
        turned[128:256, :] = swapped.reshape(768, 128).astype(BF).T

        def one(k, _):
            duo = lax.rem(gy // 2 + 1 + k, 8)
            out = dot_nn(turned[...], column_back[duo]).astype(BF)
            for j in range(2):
                target = duo * 2 + j
                back_a[step, target] = out[:, j * 128 : j * 128 + 128].reshape(2, 2, 64, 128)

                @pl.when(target == gy)
                def _():
                    pltpu.make_async_copy(
                        back_a.at[step, target], got_a.at[step, gy], ba_recv.at[step, my_half]
                    ).start()

                @pl.when(target != gy)
                def _():
                    ba_copy(step, target).start()

            return 0

        lax.fori_loop(0, 8, one, 0)

    def deep_inverse(step, xh):
        wait_all(got_a.at[step, pl.ds(xh * 8, 8)], ba_recv.at[step, xh])
        for xb in range(2):
            first = jnp.concatenate(
                [got_a[step, xh * 8 + g, p, xb, 0:48] for g in range(8) for p in range(2)], axis=0
            )
            second = jnp.concatenate(
                [got_a[step, xh * 8 + g, p, xb, 48:64] for g in range(8) for p in range(2)], axis=0
            )
            lifted[xb * 128 : xb * 128 + 128, 0:768] = first.T
            lifted[xb * 128 : xb * 128 + 128, 768:1024] = second.T

        def save(out, c):
            for j in range(2):
                branch[c + j, pl.ds(xh * 16, 16)] = (
                    out[:, j * 128 : j * 128 + 128].astype(BF).reshape(16, 16, 128)
                )

        def one(k, _):
            save(dot_nn(lifted[:, 0:768], rise0[k]), 2 * k)
            return 0

        lax.fori_loop(0, 8, one, 0)
        for k in range(2):
            save(dot_nn(lifted[:, 768:1024], rise1[k]), 16 + 2 * k)

    def pointwise(step, xh, last):
        def one(k, _):
            x = xh * 16 + k
            data = jnp.concatenate([cells[step, c, x] for c in range(C)], axis=0)
            pre = dot_nn(kron[...], data)
            for o in range(C):
                v = pre[o * 16 : o * 16 + 16] + branch[o, x].astype(F32) + bias_ref[o]
                v = v[0:15]
                square = v * v
                t = jnp.tanh(v * (GELU_K + (GELU_K * GELU_C) * square))
                half = 0.5 + 0.5 * t
                slope = half + (0.5 * v) * (1.0 - t * t) * (
                    GELU_K + (3.0 * GELU_K * GELU_C) * square
                )
                cells[step, o, x, 0:15, :] = (cots[step, o, x].astype(F32) * slope).astype(BF)
                if last:
                    act[o, x] = (v * half).astype(BF)
            return 0

        lax.fori_loop(0, 16, one, 0)

    copies[0].wait()
    pad_cells(0)
    copies[1].wait()
    copies[2].wait()
    deep_half(0, 0, 0)
    pl.semaphore_wait(barrier, GX * GY - 1)
    send_a_half(0, 0)
    deep_half(0, 0, 1)
    send_a_half(0, 1)

    copies[4].wait()
    pad_cells(1)
    deep_half(1, 1, 0)
    deep_half(1, 1, 1)

    wait_all(recv_a.at[0], a_recv.at[0])
    send_a_half(1, 0)
    send_a_half(1, 1)
    copies[3].wait()
    columns(0)
    copies[5].wait()
    copies[6].wait()
    copies[7].wait()
    wait_all(recv_b.at[0], b_recv.at[0])
    rows_forward(0)
    rows_inverse(0, mix(0, None))
    copies[8].wait()
    wait_all(got_b.at[0], bb_recv.at[0])
    columns_inverse(0)

    wait_all(recv_a.at[1], a_recv.at[1])
    columns(1)
    copies[9].wait()
    copies[10].wait()
    copies[11].wait()

    for xh in range(2):
        deep_inverse(0, xh)
        pointwise(0, xh, False)
        deep_half(2, 0, xh)
        send_a_half(2, xh)
    wait_all(recv_b.at[1], b_recv.at[1])
    rows_forward(1)
    wait_all(recv_a.at[2], a_recv.at[2])
    columns(2)
    wait_all(recv_b.at[2], b_recv.at[2])
    rows_forward(2)
    rows_inverse(1, mix(1, (0, 2)))
    wait_all(got_b.at[1], bb_recv.at[1])
    columns_inverse(1)
    for xh in range(2):
        deep_inverse(1, xh)
        pointwise(1, xh, True)
        deep_half(3, 1, xh)
        send_a_half(3, xh)
    act_out = pltpu.make_async_copy(act, act_hbm, out_sems.at[0])
    act_out.start()
    wait_all(recv_a.at[3], a_recv.at[3])
    columns(3)
    wait_all(recv_b.at[3], b_recv.at[3])
    rows_forward(3)
    mix(None, (1, 3))
    trained_out = pltpu.make_async_copy(weights, trained_hbm, out_sems.at[1])
    trained_out.start()

    for f in range(4):

        def sent_a(k, _):
            @pl.when(k != gy)
            def _():
                a_copy(f, k).wait_send()

            return 0

        lax.fori_loop(0, GY, sent_a, 0)

        def sent_b(ky, _):
            other_x, other_y, slot = b_target(ky)

            @pl.when(jnp.logical_not(jnp.logical_and(other_x == gx, other_y == gy)))
            def _():
                b_copy(f, ky).wait_send()

            return 0

        lax.fori_loop(0, KY, sent_b, 0)
    for step in range(2):

        def sent_ba(k, _):
            @pl.when(k != gy)
            def _():
                ba_copy(step, k).wait_send()

            return 0

        lax.fori_loop(0, GY, sent_ba, 0)
        for slot in range(3):
            group = gy * 3 + slot

            def sent_bb(n, _):
                mine = jnp.logical_and(
                    lax.rem(n, 8) == gx, (n // 8) * 8 + lax.rem(group, 8) == gy
                )

                @pl.when(jnp.logical_not(mine))
                def _():
                    bb_copy(step, slot, n).wait_send()

                return 0

            lax.fori_loop(0, 16, sent_bb, 0)
    act_out.wait()
    trained_out.wait()


def shards(fields, cotangents, w_point, bias_vector, spectral):
    tables = [jnp.asarray(table) for table in make_tables()]
    anywhere = pl.BlockSpec(memory_space=pl.ANY)
    vmem = pltpu.VMEM
    grid_shape = (C, 32, 15, 128)
    dma = pltpu.SemaphoreType.DMA
    scratch = [
        vmem((2,) + grid_shape, BF),
        vmem((2,) + grid_shape, BF),
        vmem((2, C, 32, 16, 128), BF),
        vmem((2, C, C, 432), F32),
        vmem(grid_shape, BF),
    ]
    scratch += [vmem(table.shape, BF) for table in tables]
    scratch += [
        vmem((4, GY, 2, 2, 64, 128), BF),
        vmem((4, GY, 2, 2, 64, 128), BF),
        vmem((4, KY, 16, 128), BF),
        vmem((4, 3, 2, GX, 16, 128), BF),
        vmem((2, 3, 16, 16, 128), BF),
        vmem((2, KY, 16, 128), BF),
        vmem((2, GY, 2, 2, 64, 128), BF),
        vmem((2, GY, 2, 2, 64, 128), BF),
        vmem((3, 64, 128), F32),
        vmem((4, 2, C, 432), F32),
        vmem((3, 64, 128), F32),
        vmem((256, 768), BF),
        vmem((256, 1024), BF),
        vmem((C, 32, 16, 128), BF),
        vmem((C * 16, C * 16), BF),
        dma((12,)),
        dma((2,)),
        dma((4,)),
        dma((4,)),
        dma((4,)),
        dma((4,)),
        dma((2,)),
        dma((2,)),
        dma((2,)),
        dma((2, 2)),
    ]
    return pl.pallas_call(
        kernel,
        out_shape=(
            jax.ShapeDtypeStruct(grid_shape, BF),
            jax.ShapeDtypeStruct((2, C, C, 432), F32),
        ),
        in_specs=[
            anywhere,
            anywhere,
            pl.BlockSpec(memory_space=pltpu.VMEM),
            pl.BlockSpec(memory_space=pltpu.SMEM),
            anywhere,
        ]
        + [anywhere] * len(tables),
        out_specs=(anywhere, anywhere),
        scratch_shapes=scratch,
        compiler_params=pltpu.CompilerParams(
            collective_id=0, has_side_effects=True, vmem_limit_bytes=62 * 1024 * 1024
        ),
    )(fields, cotangents, w_point, bias_vector, spectral, *tables)


def solution(mesh):
    return jax.shard_map(
        shards,
        mesh=mesh,
        in_specs=(
            P(None, None, "gx", "gy", None),
            P(None, None, "gx", "gy", None),
            P(),
            P(),
            P(None, None, None, ("gx", "gy")),
        ),
        out_specs=(P(None, "gx", "gy", None), P(None, None, None, ("gx", "gy"))),
        check_vma=False,
    )
```

time: 628 us -> 212 us (0.34); the launches traced: 618 us -> 211 us
  local copies, waits for them, and re-layouts: 391 us -> 21.5 us
  Pallas kernels: 0 us -> 189 us
  starting transfers between devices: 66.3 us -> 0 us
  blocking collectives: 50.6 us -> 0 us
  matrix products: 43.6 us -> 0 us
  waiting for transfers between devices: 39.3 us -> 0 us
  other arithmetic: 25.6 us -> 0.01 us
    pallas_call x0 -> x1, Pallas kernels: none -> 189 us  [shards(): pl.pallas_call(kernel, out_shape=(jax.ShapeDtypeStruct(grid_shape, BF), j...]
    reshape x28 -> x0, local copies, waits for them, and re-layouts: 158 us -> none  [the longest x8 70.9 us: spectrum(): line_modes.reshape(channels, line_rows, NY, 2, KZ)]
    unnamed x92 -> x9, local copies, waits for them, and re-layouts: 123 us -> 15.1 us
    all_to_all x9 -> x0, starting transfers between devices: 66.3 us -> none  [the longest x3 27.9 us: spectrum(): lax.all_to_all(column_modes, ('gx', 'gy'), split_axis=3, concat_axis=2, t...]
    all_to_all x3 -> x0, blocking collectives: 50.6 us -> none  [the longest x1 18.6 us: spectrum(): lax.all_to_all(depth_modes, 'gy', split_axis=1, concat_axis=2, tiled=True)]
    all_to_all x14 -> x0, local copies, waits for them, and re-layouts: 47.6 us -> none  [the longest x4 26.4 us: spectrum(): lax.all_to_all(depth_modes, 'gy', split_axis=1, concat_axis=2, tiled=True)]
    dot_general x20 -> x0, matrix products: 43.6 us -> none  [the longest x2 11.5 us: shards(): jnp.einsum('oi,ixyz->oxyz', w_point, field_cells, preferred_element_type=...]
    all_to_all x9 -> x0, waiting for transfers between devices: 39.3 us -> none  [the longest x3 19.6 us: spectrum(): lax.all_to_all(column_modes, ('gx', 'gy'), split_axis=3, concat_axis=2, t...]
  transfers between devices with their start and end apart: 9 -> 0, of which waited for: 5 -> 0; matrix products, arithmetic and copies ran while one was open for 30% -> 0% of each run, Pallas kernels for 0% -> 0%
where the time goes in v2:
time: 212 us; the launch traced here: 211 us
  Pallas kernels  189 us (89%)
  local copies, waits for them, and re-layouts  21.5 us (10%)
    pallas_call x1, Pallas kernels, shards(): pl.pallas_call(kernel, out_shape=(jax.ShapeDtypeStruct(grid_shape, BF), j...  189 us
    unnamed x9, local copies, waits for them, and re-layouts  15.1 us
    pallas_call x2, local copies, waits for them, and re-layouts, shards(): pl.pallas_call(kernel, out_shape=(jax.ShapeDtypeStruct(grid_shape, BF), j...  6.41 us

profile of v2, /device:TPU:1, one launch (start us, length us, event | category | flops | bytes accessed | tf_op | source)
XLA Modules:
  0.0 211.4 jit_solution(12611699664722625329)
XLA Ops:
  0.6 0.0 slice-start
  0.6 3.2 %copy.17.spectral_hbm = f32[2,20,20,432]{3,2,1,0:T(8,128)} copy(f32[2,20,20,432]{3,0,2,1:T(2,128)} %param.17) | data formatting | bytes 2764800 | tf_op args[4]
  3.8 0.0 slice-start.1
  3.8 7.1 %copy.15.fields_hbm = bf16[2,20,32,15,128]{4,3,2,1,0:T(8,128)(2,1)} copy(bf16[2,20,32,15,128]{4,2,3,1,0:T(8,128)(2,1)} %param.13) | data formatting | bytes 9830400 | tf_op args[0]
  11.0 0.0 slice-done
  11.0 0.0 slice-done.1
  11.0 4.7 %copy.16.cots_hbm = bf16[2,20,32,15,128]{4,3,2,1,0:T(8,128)(2,1)} copy(bf16[2,20,32,15,128]{4,2,3,1,0:T(8,128)(2,1)S(1)} %bitcast.1) | data formatting | bytes 9830400 | tf_op args[1]
  15.7 189.3 %shard_map.140 = (bf16[20,32,15,128]{3,2,1,0:T(8,128)(2,1)}, f32[2,20,20,432]{3,2,1,0:T(8,128)}) custom-call(bf16[2,20,32,15,128]{4,3,2,1,0:T(8,128)(2,1)} %copy.15.fields_hbm, bf16[2,20,32,15,128]{4,3,2,1,0:T(8,128)(2,1)} %copy.16.cots_hbm, bf16[20,20]{1,0:T(8,128)(2,1)} %w_ref.1, f32[20]{0:T(128)} %bias_ref.1, f32[2,20,20,432]{3,2,1,0:T(8,128)} %copy.17.spectral_hbm, ...), custom_call_target="tpu_custom_call" | custom-call | tf_op jit(solution)/shard_map/pallas_call | solution.py:606
  205.0 0.0 copy-start
  205.0 4.0 %copy.18 = bf16[20,32,15,128]{3,1,2,0:T(8,128)(2,1)} copy(bf16[20,32,15,128]{3,2,1,0:T(8,128)(2,1)} %get-tuple-element.2) | data formatting | bytes 4915200 | tf_op jit(solution)/shard_map/pallas_call | solution.py:606
  209.0 0.0 copy-done
  209.0 2.4 %copy.19 = f32[2,20,20,432]{3,0,2,1:T(2,128)} copy(f32[2,20,20,432]{3,2,1,0:T(8,128)S(1)} %copy-done) | data formatting | bytes 2764800 | tf_op jit(solution)/shard_map/pallas_call | solution.py:606
  (1 shorter events, 0.0 us)
Async XLA Ops:
  0.6 10.4 %slice-start = ((s8[4915200]{0:T(1024)(128)(4,1)}), s8[4194304]{0:T(1024)(128)(4,1)S(1)}, s32[]{:S(2)}) async-start(s8[4915200]{0:T(1024)(128)(4,1)} %bitcast), calls=%async_computation | async-start | bytes 8388608
  3.8 7.2 %slice-start.1 = ((s8[4915200]{0:T(1024)(128)(4,1)}), s8[720896]{0:T(1024)(128)(4,1)S(1)}, s32[]{:S(2)}) async-start(s8[4915200]{0:T(1024)(128)(4,1)} %bitcast), calls=%async_computation.1 | async-start | bytes 1441792
  205.0 4.0 %copy-start = (f32[2,20,20,432]{3,2,1,0:T(8,128)S(1)}, f32[2,20,20,432]{3,2,1,0:T(8,128)}, u32[]{:S(2)}) copy-start(f32[2,20,20,432]{3,2,1,0:T(8,128)} %get-tuple-element.3) | copy-start | bytes 4147204

commit v3 on v2

--- a/solution.py
+++ b/solution.py
@@ -62,10 +62,10 @@
     padded = np.zeros((2, GY, 16, KY), np.float32)
     padded[:, :, :15] = np.stack([cos_y, sin_y]).reshape(2, GY, 15, KY)
     eye8 = np.eye(8, dtype=np.float32)
-    column = np.einsum("asyk,xw->akxswy", padded, eye8)
+    column = np.einsum("asyk,xw->akxsyw", padded, eye8)
     column = column.reshape(2, 2, 24 * 8, 2048).transpose(1, 0, 2, 3).reshape(2, 384, 2048)
     signed = np.stack([padded[0], -padded[1]])
-    column_back = np.einsum("asyk,wx->kawsxy", signed, eye8)
+    column_back = np.einsum("asyk,wx->kawsyx", signed, eye8)
     column_back = column_back.reshape(768, 8, 256).transpose(1, 0, 2)
     cos_x, sin_x = angle_tables(NX, waves(NX, KX))
     shape = (GX, 2, 2, 8, KX)
@@ -111,7 +111,7 @@
     fields_hbm, cots_hbm, w_ref, bias_ref, spectral_hbm,
     deep0_hbm, deep1_hbm, column_hbm, row_hbm, row_back_hbm, column_back_hbm, rise0_hbm, rise1_hbm,
     act_hbm, trained_hbm,
-    fields, cots, cells, weights, act,
+    fields, cots, cells, packed, weights, act,
     deep0, deep1, column, row, row_back, column_back, rise0, rise1,
     send_a, recv_a, send_b, recv_b, back_b, got_b, back_a, got_a,
     xs, spectra, xi, turned, lifted, branch, kron,
@@ -125,24 +125,27 @@
     my_group = gy % 8
 
     loads = [
-        (fields_hbm.at[0], fields.at[0]),
+        (fields_hbm.at[0], fields.at[0, :, pl.ds(0, 15)]),
         (deep0_hbm, deep0),
         (deep1_hbm, deep1),
         (column_hbm, column),
-        (fields_hbm.at[1], fields.at[1]),
+        (fields_hbm.at[1], fields.at[1, :, pl.ds(0, 15)]),
         (row_hbm, row),
-        (spectral_hbm, weights),
+        (spectral_hbm, packed),
         (row_back_hbm, row_back),
         (column_back_hbm, column_back),
         (rise0_hbm, rise0),
         (rise1_hbm, rise1),
-        (cots_hbm, cots),
+        (cots_hbm, cots.at[:, :, pl.ds(0, 15)]),
     ]
     copies = [
         pltpu.make_async_copy(src, dst, load_sems.at[n]) for n, (src, dst) in enumerate(loads)
     ]
-    for copy in copies:
+    for copy in copies[:3]:
         copy.start()
+    for step in range(2):
+        fields[step, :, 15] = jnp.zeros((C, 32, 128), BF)
+        cots[step, :, 15] = jnp.zeros((C, 32, 128), BF)
 
     barrier = pltpu.get_barrier_semaphore()
 
@@ -165,20 +168,18 @@
     xi[...] = jnp.zeros_like(xi)
 
     def pad_cells(step):
-        cells[step] = jnp.zeros((C, 32, 16, 128), BF)
-
         def one(c, _):
-            cells[step, c, :, 0:15, :] = fields[step, c]
+            value = fields[step, c].astype(F32).reshape(16, 4, 8, 128)
+            for block in range(4):
+                cells[step, c, block] = value[:, block].reshape(128, 128).astype(BF)
             return 0
 
         lax.fori_loop(0, C, one, 0)
 
     def deep_half(f, step, xh):
         for xb in range(2):
-            rows = pl.ds((xh * 2 + xb) * 8, 8)
-
             def block(c):
-                return cells[step, c, rows].reshape(128, 128)
+                return cells[step, c, xh * 2 + xb]
 
             o0 = dot_nt(deep0[...], jnp.concatenate([block(c) for c in range(8)], axis=1))
             o1 = dot_nt(deep0[...], jnp.concatenate([block(c) for c in range(8, 16)], axis=1))
@@ -414,8 +415,8 @@
 
         def save(out, c):
             for j in range(2):
-                branch[c + j, pl.ds(xh * 16, 16)] = (
-                    out[:, j * 128 : j * 128 + 128].astype(BF).reshape(16, 16, 128)
+                branch[c + j, pl.ds(xh * 2, 2)] = (
+                    out[:, j * 128 : j * 128 + 128].astype(BF).reshape(2, 128, 128)
                 )
 
         def one(k, _):
@@ -428,102 +429,51 @@
 
     def pointwise(step, xh, last):
         def one(k, _):
-            x = xh * 16 + k
-            data = jnp.concatenate([cells[step, c, x] for c in range(C)], axis=0)
+            rows = pl.ds(k * 16, 16)
+            data = jnp.concatenate(
+                [
+                    jnp.concatenate([cells[step, c, xh * 2 + xb, rows] for c in range(C)], axis=0)
+                    for xb in range(2)
+                ],
+                axis=1,
+            )
             pre = dot_nn(kron[...], data)
             for o in range(C):
-                v = pre[o * 16 : o * 16 + 16] + branch[o, x].astype(F32) + bias_ref[o]
-                v = v[0:15]
-                square = v * v
-                t = jnp.tanh(v * (GELU_K + (GELU_K * GELU_C) * square))
-                half = 0.5 + 0.5 * t
-                slope = half + (0.5 * v) * (1.0 - t * t) * (
-                    GELU_K + (3.0 * GELU_K * GELU_C) * square
-                )
-                cells[step, o, x, 0:15, :] = (cots[step, o, x].astype(F32) * slope).astype(BF)
+                cot = cots[step, o, pl.ds(2 * k, 2), xh * 16 : xh * 16 + 16].astype(F32)
+                cot = cot.reshape(2, 2, 8, 128)
+                outs = []
+                for xb in range(2):
+                    v = pre[o * 16 : o * 16 + 16, xb * 128 : xb * 128 + 128]
+                    v = v + (branch[o, xh * 2 + xb, rows].astype(F32) + bias_ref[o])
+                    square = v * v
+                    half = 0.5 + 0.5 * jnp.tanh(v * (GELU_K + (GELU_K * GELU_C) * square))
+                    slope = half + (half * (1.0 - half)) * (
+                        v * (2.0 * GELU_K + (6.0 * GELU_K * GELU_C) * square)
+                    )
+                    cells[step, o, xh * 2 + xb, rows] = (
+                        cot[:, xb].reshape(16, 128) * slope
+                    ).astype(BF)
+                    outs.append((v * half).reshape(2, 8, 128))
                 if last:
-                    act[o, x] = (v * half).astype(BF)
-            return 0
-
-        lax.fori_loop(0, 16, one, 0)
-
-    copies[0].wait()
-    pad_cells(0)
-    copies[1].wait()
-    copies[2].wait()
-    deep_half(0, 0, 0)
-    pl.semaphore_wait(barrier, GX * GY - 1)
-    send_a_half(0, 0)
-    deep_half(0, 0, 1)
-    send_a_half(0, 1)
-
-    copies[4].wait()
-    pad_cells(1)
-    deep_half(1, 1, 0)
-    deep_half(1, 1, 1)
-
-    wait_all(recv_a.at[0], a_recv.at[0])
-    send_a_half(1, 0)
-    send_a_half(1, 1)
-    copies[3].wait()
-    columns(0)
-    copies[5].wait()
-    copies[6].wait()
-    copies[7].wait()
-    wait_all(recv_b.at[0], b_recv.at[0])
-    rows_forward(0)
-    rows_inverse(0, mix(0, None))
-    copies[8].wait()
-    wait_all(got_b.at[0], bb_recv.at[0])
-    columns_inverse(0)
-
-    wait_all(recv_a.at[1], a_recv.at[1])
-    columns(1)
-    copies[9].wait()
-    copies[10].wait()
-    copies[11].wait()
-
-    for xh in range(2):
-        deep_inverse(0, xh)
-        pointwise(0, xh, False)
-        deep_half(2, 0, xh)
-        send_a_half(2, xh)
-    wait_all(recv_b.at[1], b_recv.at[1])
-    rows_forward(1)
-    wait_all(recv_a.at[2], a_recv.at[2])
-    columns(2)
-    wait_all(recv_b.at[2], b_recv.at[2])
-    rows_forward(2)
-    rows_inverse(1, mix(1, (0, 2)))
-    wait_all(got_b.at[1], bb_recv.at[1])
-    columns_inverse(1)
-    for xh in range(2):
-        deep_inverse(1, xh)
-        pointwise(1, xh, True)
-        deep_half(3, 1, xh)
-        send_a_half(3, xh)
-    act_out = pltpu.make_async_copy(act, act_hbm, out_sems.at[0])
-    act_out.start()
-    wait_all(recv_a.at[3], a_recv.at[3])
-    columns(3)
-    wait_all(recv_b.at[3], b_recv.at[3])
-    rows_forward(3)
-    mix(None, (1, 3))
-    trained_out = pltpu.make_async_copy(weights, trained_hbm, out_sems.at[1])
-    trained_out.start()
-
-    for f in range(4):
-
-        def sent_a(k, _):
+                    act[o, pl.ds(2 * k, 2), xh * 16 : xh * 16 + 16] = jnp.concatenate(
+                        outs, axis=1
+                    ).astype(BF)
+            return 0
+
+        lax.fori_loop(0, 8, one, 0)
+
+    def all_a_sent(f):
+        def one(k, _):
             @pl.when(k != gy)
             def _():
                 a_copy(f, k).wait_send()
 
             return 0
 
-        lax.fori_loop(0, GY, sent_a, 0)
-
-        def sent_b(ky, _):
+        lax.fori_loop(0, GY, one, 0)
+
+    def all_b_sent(f):
+        def one(ky, _):
             other_x, other_y, slot = b_target(ky)
 
             @pl.when(jnp.logical_not(jnp.logical_and(other_x == gx, other_y == gy)))
@@ -532,21 +482,23 @@
 
             return 0
 
-        lax.fori_loop(0, KY, sent_b, 0)
-    for step in range(2):
-
-        def sent_ba(k, _):
+        lax.fori_loop(0, KY, one, 0)
+
+    def all_ba_sent(step):
+        def one(k, _):
             @pl.when(k != gy)
             def _():
                 ba_copy(step, k).wait_send()
 
             return 0
 
-        lax.fori_loop(0, GY, sent_ba, 0)
+        lax.fori_loop(0, GY, one, 0)
+
+    def all_bb_sent(step):
         for slot in range(3):
             group = gy * 3 + slot
 
-            def sent_bb(n, _):
+            def one(n, _):
                 mine = jnp.logical_and(
                     lax.rem(n, 8) == gx, (n // 8) * 8 + lax.rem(group, 8) == gy
                 )
@@ -557,8 +509,133 @@
 
                 return 0
 
-            lax.fori_loop(0, 16, sent_bb, 0)
-    act_out.wait()
+            lax.fori_loop(0, 16, one, 0)
+
+    def mix_and_return(step, f, update):
+        rows_inverse(step, mix(f, update))
+
+    def wait_a(f):
+        wait_all(recv_a.at[f], a_recv.at[f])
+
+    def wait_b(f):
+        wait_all(recv_b.at[f], b_recv.at[f])
+
+    def wait_bb(step):
+        wait_all(got_b.at[step], bb_recv.at[step])
+
+    def start():
+        copies[0].wait()
+        for copy in copies[3:]:
+            copy.start()
+        pad_cells(0)
+        copies[1].wait()
+        copies[2].wait()
+
+    def unpack_weights():
+        def one(i, _):
+            for part in range(2):
+                weights[part, i] = packed[i, :, part, :]
+            return 0
+
+        lax.fori_loop(0, C, one, 0)
+
+    def pack_weights():
+        def one(i, _):
+            for part in range(2):
+                packed[i, :, part, :] = weights[part, i]
+            return 0
+
+        lax.fori_loop(0, C, one, 0)
+
+    def meet():
+        pl.semaphore_wait(barrier, GX * GY - 1)
+
+    def load_second():
+        copies[4].wait()
+        pad_cells(1)
+
+    def loaded(*numbers):
+        for n in numbers:
+            copies[n].wait()
+
+    def act_copy():
+        return pltpu.make_async_copy(act.at[:, pl.ds(0, 15)], act_hbm, out_sems.at[0])
+
+    def act_start():
+        act_copy().start()
+
+    schedule = [
+        (start,),
+        (deep_half, 0, 0, 0),
+        (meet,),
+        (send_a_half, 0, 0),
+        (deep_half, 0, 0, 1),
+        (send_a_half, 0, 1),
+        (load_second,),
+        (deep_half, 1, 1, 0),
+        (deep_half, 1, 1, 1),
+        (loaded, 6),
+        (unpack_weights,),
+        (wait_a, 0),
+        (send_a_half, 1, 0),
+        (send_a_half, 1, 1),
+        (loaded, 3),
+        (columns, 0),
+        (loaded, 5, 7),
+        (wait_b, 0),
+        (rows_forward, 0),
+        (mix_and_return, 0, 0, None),
+        (loaded, 8),
+        (wait_bb, 0),
+        (columns_inverse, 0),
+        (wait_a, 1),
+        (columns, 1),
+        (loaded, 9, 10, 11),
+        (deep_inverse, 0, 0),
+        (pointwise, 0, 0, False),
+        (deep_half, 2, 0, 0),
+        (send_a_half, 2, 0),
+        (deep_inverse, 0, 1),
+        (pointwise, 0, 1, False),
+        (deep_half, 2, 0, 1),
+        (send_a_half, 2, 1),
+        (wait_b, 1),
+        (rows_forward, 1),
+        (wait_a, 2),
+        (columns, 2),
+        (wait_b, 2),
+        (rows_forward, 2),
+        (mix_and_return, 1, 1, (0, 2)),
+        (wait_bb, 1),
+        (columns_inverse, 1),
+        (deep_inverse, 1, 0),
+        (pointwise, 1, 0, True),
+        (deep_half, 3, 1, 0),
+        (send_a_half, 3, 0),
+        (deep_inverse, 1, 1),
+        (pointwise, 1, 1, True),
+        (deep_half, 3, 1, 1),
+        (send_a_half, 3, 1),
+        (act_start,),
+        (wait_a, 3),
+        (columns, 3),
+        (wait_b, 3),
+        (rows_forward, 3),
+        (mix, None, (1, 3)),
+        (pack_weights,),
+    ]
+    for stage, *numbers in schedule:
+        stage(*numbers)
+    trained_out = pltpu.make_async_copy(packed, trained_hbm, out_sems.at[1])
+    trained_out.start()
+
+    for f in range(4):
+        all_a_sent(f)
+        all_b_sent(f)
+    for step in range(2):
+        all_ba_sent(step)
+        all_bb_sent(step)
+    act_copy().wait()
     trained_out.wait()
 
 
@@ -566,12 +643,16 @@
     tables = [jnp.asarray(table) for table in make_tables()]
     anywhere = pl.BlockSpec(memory_space=pl.ANY)
     vmem = pltpu.VMEM
-    grid_shape = (C, 32, 15, 128)
+    fields = jnp.transpose(fields, (0, 1, 3, 2, 4))
+    cotangents = jnp.transpose(cotangents, (0, 1, 3, 2, 4))
+    spectral = jnp.transpose(spectral, (1, 2, 0, 3))
+    grid_shape = (C, 16, 32, 128)
     dma = pltpu.SemaphoreType.DMA
     scratch = [
         vmem((2,) + grid_shape, BF),
         vmem((2,) + grid_shape, BF),
-        vmem((2, C, 32, 16, 128), BF),
+        vmem((2, C, 4, 128, 128), BF),
+        vmem((C, C, 2, 432), F32),
         vmem((2, C, C, 432), F32),
         vmem(grid_shape, BF),
     ]
@@ -590,7 +671,7 @@
         vmem((3, 64, 128), F32),
         vmem((256, 768), BF),
         vmem((256, 1024), BF),
-        vmem((C, 32, 16, 128), BF),
+        vmem((C, 4, 128, 128), BF),
         vmem((C * 16, C * 16), BF),
         dma((12,)),
         dma((2,)),
@@ -603,11 +684,11 @@
         dma((2,)),
         dma((2, 2)),
     ]
-    return pl.pallas_call(
+    act, trained = pl.pallas_call(
         kernel,
         out_shape=(
-            jax.ShapeDtypeStruct(grid_shape, BF),
-            jax.ShapeDtypeStruct((2, C, C, 432), F32),
+            jax.ShapeDtypeStruct((C, 15, 32, 128), BF),
+            jax.ShapeDtypeStruct((C, C, 2, 432), F32),
         ),
         in_specs=[
             anywhere,
@@ -623,6 +704,7 @@
             collective_id=0, has_side_effects=True, vmem_limit_bytes=62 * 1024 * 1024
         ),
     )(fields, cotangents, w_point, bias_vector, spectral, *tables)
+    return jnp.transpose(act, (0, 2, 1, 3)), jnp.transpose(trained, (2, 0, 1, 3))
 
 
 def solution(mesh):

time: 212 us -> 187 us (0.88)
  local copies, waits for them, and re-layouts: 21.5 us -> 4.84 us
  Pallas kernels: 189 us -> 181 us
    unnamed x9 -> x4, local copies, waits for them, and re-layouts: 15.1 us -> 4.84 us
    pallas_call x1, Pallas kernels: 189 us -> 181 us  [shards(): pl.pallas_call(kernel, out_shape=(jax.ShapeDtypeStruct((C, 15, 32, 128),...]
    pallas_call x2 -> x0, local copies, waits for them, and re-layouts: 6.41 us -> none  [shards(): pl.pallas_call(kernel, out_shape=(jax.ShapeDtypeStruct(grid_shape, BF), j...]
where the time goes in v3:
time: 187 us; the launch traced here: 186 us
  Pallas kernels  181 us (97%)
  local copies, waits for them, and re-layouts  4.84 us (3%)
    pallas_call x1, Pallas kernels, shards(): pl.pallas_call(kernel, out_shape=(jax.ShapeDtypeStruct((C, 15, 32, 128),...  181 us
    unnamed x4, local copies, waits for them, and re-layouts  4.84 us

profile of v3, /device:TPU:1, one launch (start us, length us, event | category | flops | bytes accessed | tf_op | source)
XLA Modules:
  0.0 186.2 jit_solution(16571750687921923487)
XLA Ops:
  0.6 180.7 %shard_map.140 = (bf16[20,15,32,128]{3,2,1,0:T(8,128)(2,1)}, f32[20,20,2,432]{3,2,1,0:T(2,128)}) custom-call(bf16[2,20,15,32,128]{4,3,2,1,0:T(8,128)(2,1)} %bitcast.5, bf16[2,20,15,32,128]{4,3,2,1,0:T(8,128)(2,1)} %bitcast.6, bf16[20,20]{1,0:T(8,128)(2,1)} %w_ref.1, f32[20]{0:T(128)} %bias_ref.1, f32[20,20,2,432]{3,2,1,0:T(2,128)} %bitcast.8, ...), custom_call_target="tpu_custom_call" | custom-call | tf_op jit(solution)/shard_map/pallas_call | solution.py:687
  181.4 0.0 copy-start
  181.4 3.7 %copy.17 = bf16[20,32,15,128]{3,1,2,0:T(8,128)(2,1)} copy(bf16[20,32,15,128]{3,1,2,0:T(8,128)(2,1)} %bitcast.7) | data formatting | bytes 4915200
  185.1 0.0 copy-done
  185.1 1.2 copy.18
Async XLA Ops:
  181.4 3.7 %copy-start = (f32[20,20,2,432]{3,2,1,0:T(2,128)S(1)}, f32[20,20,2,432]{3,2,1,0:T(2,128)}, u32[]{:S(2)}) copy-start(f32[20,20,2,432]{3,2,1,0:T(2,128)} %get-tuple-element.5) | copy-start | bytes 4147204

commit v4 on v3

--- a/solution.py
+++ b/solution.py
@@ -69,8 +69,8 @@
     column_back = column_back.reshape(768, 8, 256).transpose(1, 0, 2)
     cos_x, sin_x = angle_tables(NX, waves(NX, KX))
     shape = (GX, 2, 2, 8, KX)
-    cos_x = cos_x.reshape(shape).transpose(1, 0, 2, 3, 4)
-    sin_x = sin_x.reshape(shape).transpose(1, 0, 2, 3, 4)
+    cos_x = cos_x.reshape(shape).transpose(2, 0, 1, 3, 4)
+    sin_x = sin_x.reshape(shape).transpose(2, 0, 1, 3, 4)
     row = np.zeros((2, GX, 2, 8, 2, 2, 64), np.float32)
     row_back = np.zeros_like(row)
     for xb in range(2):
@@ -115,7 +115,7 @@
     deep0, deep1, column, row, row_back, column_back, rise0, rise1,
     send_a, recv_a, send_b, recv_b, back_b, got_b, back_a, got_a,
     xs, spectra, xi, turned, lifted, branch, kron,
-    load_sems, out_sems,
+    load_sems, out_sems, complete,
     a_send, a_recv, b_send, b_recv, bb_send, bb_recv, ba_send, ba_recv,
 ):
     gx = lax.axis_index("gx")
@@ -125,7 +125,7 @@
     my_group = gy % 8
 
     loads = [
-        (fields_hbm.at[0], fields.at[0, :, pl.ds(0, 15)]),
+        (fields_hbm.at[0, :, :, pl.ds(0, 16)], fields.at[0, :, pl.ds(0, 15), pl.ds(0, 16)]),
         (deep0_hbm, deep0),
         (deep1_hbm, deep1),
         (column_hbm, column),
@@ -137,26 +137,33 @@
         (rise0_hbm, rise0),
         (rise1_hbm, rise1),
         (cots_hbm, cots.at[:, :, pl.ds(0, 15)]),
+        (fields_hbm.at[0, :, :, pl.ds(16, 16)], fields.at[0, :, pl.ds(0, 15), pl.ds(16, 16)]),
     ]
     copies = [
         pltpu.make_async_copy(src, dst, load_sems.at[n]) for n, (src, dst) in enumerate(loads)
     ]
-    for copy in copies[:3]:
-        copy.start()
+    for n in (0, 1, 2, 12):
+        copies[n].start()
     for step in range(2):
         fields[step, :, 15] = jnp.zeros((C, 32, 128), BF)
         cots[step, :, 15] = jnp.zeros((C, 32, 128), BF)
 
     barrier = pltpu.get_barrier_semaphore()
 
-    def greet(d, _):
-        other = lax.rem(me + d, GX * GY)
+    def greet_line(d, _):
         pl.semaphore_signal(
-            barrier, inc=1, device_id=(other // GY, lax.rem(other, GY)), device_id_type=MESH
+            barrier, inc=1, device_id=(gx, lax.rem(gy + d, GY)), device_id_type=MESH
         )
         return 0
 
-    lax.fori_loop(1, GX * GY, greet, 0)
+    def greet_plane(d, _):
+        pl.semaphore_signal(
+            barrier, inc=1, device_id=(lax.rem(gx + d, GX), gy), device_id_type=MESH
+        )
+        return 0
+
+    lax.fori_loop(1, GY, greet_line, 0)
+    lax.fori_loop(1, GX, greet_plane, 0)
 
     wide = lax.broadcasted_iota(jnp.int32, (C * 16, C), 0) // 16
     spread = (wide == lax.broadcasted_iota(jnp.int32, (C * 16, C), 1)).astype(BF)
@@ -167,19 +174,19 @@
     kron[...] = jnp.where(same, grown, 0.0).astype(BF)
     xi[...] = jnp.zeros_like(xi)
 
-    def pad_cells(step):
+    def pad_cells(step, xb):
         def one(c, _):
-            value = fields[step, c].astype(F32).reshape(16, 4, 8, 128)
-            for block in range(4):
-                cells[step, c, block] = value[:, block].reshape(128, 128).astype(BF)
+            value = fields[step, c, :, xb * 16 : xb * 16 + 16].astype(F32).reshape(16, 2, 8, 128)
+            for xh in range(2):
+                cells[step, c, xb * 2 + xh] = value[:, xh].reshape(128, 128).astype(BF)
             return 0
 
         lax.fori_loop(0, C, one, 0)
 
-    def deep_half(f, step, xh):
-        for xb in range(2):
+    def deep_half(f, step, xb):
+        for xh in range(2):
             def block(c):
-                return cells[step, c, xh * 2 + xb]
+                return cells[step, c, xb * 2 + xh]
 
             o0 = dot_nt(deep0[...], jnp.concatenate([block(c) for c in range(8)], axis=1))
             o1 = dot_nt(deep0[...], jnp.concatenate([block(c) for c in range(8, 16)], axis=1))
@@ -188,35 +195,27 @@
                 for part in range(2):
                     a = group * 48 + part * 24
                     b = group * 32 + part * 16
-                    send_a[f, xh * 8 + group, part, xb] = jnp.concatenate(
+                    send_a[f, xb, xh * 8 + group, part] = jnp.concatenate(
                         [o0[a : a + 24], o1[a : a + 24], o2[b : b + 16]], axis=0
                     ).astype(BF)
 
-    def a_copy(f, target):
+    def a_copy(f, xb, target):
         return pltpu.make_async_remote_copy(
-            src_ref=send_a.at[f, target],
-            dst_ref=recv_a.at[f, gy],
+            src_ref=send_a.at[f, xb, target],
+            dst_ref=recv_a.at[f, xb, gy],
             send_sem=a_send.at[f],
             recv_sem=a_recv.at[f],
             device_id=(gx, target),
             device_id_type=MESH,
         )
 
-    def send_a_half(f, xh):
+    def send_a_half(f, xb):
         def one(k, _):
-            target = xh * 8 + lax.rem(my_group + 1 + k, 8)
-
-            @pl.when(target == gy)
-            def _():
-                pltpu.make_async_copy(send_a.at[f, target], recv_a.at[f, gy], a_recv.at[f]).start()
-
-            @pl.when(target != gy)
-            def _():
-                a_copy(f, target).start()
-
-            return 0
-
-        lax.fori_loop(0, 8, one, 0)
+            a_copy(f, xb, lax.rem(gy + k, GY)).start()
+            return 0
+
+        lax.fori_loop(1, GY, one, 0)
+        pltpu.make_async_copy(send_a.at[f, xb, gy], recv_a.at[f, xb, gy], a_recv.at[f]).start()
 
     def wait_all(ref, sem):
         pltpu.make_async_copy(ref, ref, sem).wait()
@@ -238,7 +237,13 @@
 
     def columns(f):
         data = jnp.concatenate(
-            [recv_a[f, s].reshape(256, 128) for s in range(GY)], axis=1
+            [
+                jnp.concatenate(
+                    [recv_a[f, xb, s, p] for p in range(2) for xb in range(2)], axis=0
+                )
+                for s in range(GY)
+            ],
+            axis=1,
         )
         for part in range(2):
             out = dot_nt(column[part], data)
@@ -364,15 +369,33 @@
 
             lax.fori_loop(0, 16, one, 0)
 
-    def ba_copy(step, target):
+    def ba_copy(step, xb, target):
         return pltpu.make_async_remote_copy(
-            src_ref=back_a.at[step, target],
-            dst_ref=got_a.at[step, gy],
+            src_ref=back_a.at[step, xb, target],
+            dst_ref=got_a.at[step, xb, gy],
             send_sem=ba_send.at[step],
-            recv_sem=ba_recv.at[step, my_half],
+            recv_sem=ba_recv.at[step, xb],
             device_id=(gx, target),
             device_id_type=MESH,
         )
+
+    def send_ba(step, xb, target):
+        @pl.when(target == gy)
+        def _():
+            pltpu.make_async_copy(
+                back_a.at[step, xb, target], got_a.at[step, xb, gy], ba_recv.at[step, xb]
+            ).start()
+
+        @pl.when(target != gy)
+        def _():
+            ba_copy(step, xb, target).start()
+
+    def send_ba_half(step, xb):
+        def one(k, _):
+            send_ba(step, xb, lax.rem(gy + 1 + k, GY))
+            return 0
+
+        lax.fori_loop(0, GY, one, 0)
 
     def columns_inverse(step):
         data = got_b[step].astype(F32)
@@ -385,37 +408,26 @@
             out = dot_nn(turned[...], column_back[duo]).astype(BF)
             for j in range(2):
                 target = duo * 2 + j
-                back_a[step, target] = out[:, j * 128 : j * 128 + 128].reshape(2, 2, 64, 128)
-
-                @pl.when(target == gy)
-                def _():
-                    pltpu.make_async_copy(
-                        back_a.at[step, target], got_a.at[step, gy], ba_recv.at[step, my_half]
-                    ).start()
-
-                @pl.when(target != gy)
-                def _():
-                    ba_copy(step, target).start()
-
+                value = out[:, j * 128 : j * 128 + 128].reshape(2, 2, 64, 128)
+                for xb in range(2):
+                    back_a[step, xb, target] = value[:, xb]
+                send_ba(step, 0, target)
             return 0
 
         lax.fori_loop(0, 8, one, 0)
 
-    def deep_inverse(step, xh):
-        wait_all(got_a.at[step, pl.ds(xh * 8, 8)], ba_recv.at[step, xh])
-        for xb in range(2):
-            first = jnp.concatenate(
-                [got_a[step, xh * 8 + g, p, xb, 0:48] for g in range(8) for p in range(2)], axis=0
-            )
-            second = jnp.concatenate(
-                [got_a[step, xh * 8 + g, p, xb, 48:64] for g in range(8) for p in range(2)], axis=0
-            )
-            lifted[xb * 128 : xb * 128 + 128, 0:768] = first.T
-            lifted[xb * 128 : xb * 128 + 128, 768:1024] = second.T
+    def deep_inverse(step, xb):
+        wait_all(got_a.at[step, xb], ba_recv.at[step, xb])
+        for xh in range(2):
+            sources = [(xh * 8 + g, p) for g in range(8) for p in range(2)]
+            first = jnp.concatenate([got_a[step, xb, t, p, 0:48] for t, p in sources], axis=0)
+            second = jnp.concatenate([got_a[step, xb, t, p, 48:64] for t, p in sources], axis=0)
+            lifted[xh * 128 : xh * 128 + 128, 0:768] = first.T
+            lifted[xh * 128 : xh * 128 + 128, 768:1024] = second.T
 
         def save(out, c):
             for j in range(2):
-                branch[c + j, pl.ds(xh * 2, 2)] = (
+                branch[c + j, pl.ds(xb * 2, 2)] = (
                     out[:, j * 128 : j * 128 + 128].astype(BF).reshape(2, 128, 128)
                 )
 
@@ -427,35 +439,35 @@
         for k in range(2):
             save(dot_nn(lifted[:, 768:1024], rise1[k]), 16 + 2 * k)
 
-    def pointwise(step, xh, last):
+    def pointwise(step, part, last):
         def one(k, _):
             rows = pl.ds(k * 16, 16)
             data = jnp.concatenate(
                 [
-                    jnp.concatenate([cells[step, c, xh * 2 + xb, rows] for c in range(C)], axis=0)
-                    for xb in range(2)
+                    jnp.concatenate([cells[step, c, part * 2 + xh, rows] for c in range(C)], axis=0)
+                    for xh in range(2)
                 ],
                 axis=1,
             )
             pre = dot_nn(kron[...], data)
             for o in range(C):
-                cot = cots[step, o, pl.ds(2 * k, 2), xh * 16 : xh * 16 + 16].astype(F32)
+                cot = cots[step, o, pl.ds(2 * k, 2), part * 16 : part * 16 + 16].astype(F32)
                 cot = cot.reshape(2, 2, 8, 128)
                 outs = []
-                for xb in range(2):
-                    v = pre[o * 16 : o * 16 + 16, xb * 128 : xb * 128 + 128]
-                    v = v + (branch[o, xh * 2 + xb, rows].astype(F32) + bias_ref[o])
+                for xh in range(2):
+                    v = pre[o * 16 : o * 16 + 16, xh * 128 : xh * 128 + 128]
+                    v = v + (branch[o, part * 2 + xh, rows].astype(F32) + bias_ref[o])
                     square = v * v
                     half = 0.5 + 0.5 * jnp.tanh(v * (GELU_K + (GELU_K * GELU_C) * square))
                     slope = half + (half * (1.0 - half)) * (
                         v * (2.0 * GELU_K + (6.0 * GELU_K * GELU_C) * square)
                     )
-                    cells[step, o, xh * 2 + xb, rows] = (
-                        cot[:, xb].reshape(16, 128) * slope
+                    cells[step, o, part * 2 + xh, rows] = (
+                        cot[:, xh].reshape(16, 128) * slope
                     ).astype(BF)
                     outs.append((v * half).reshape(2, 8, 128))
                 if last:
-                    act[o, pl.ds(2 * k, 2), xh * 16 : xh * 16 + 16] = jnp.concatenate(
+                    act[o, pl.ds(2 * k, 2), part * 16 : part * 16 + 16] = jnp.concatenate(
                         outs, axis=1
                     ).astype(BF)
             return 0
@@ -464,13 +476,11 @@
 
     def all_a_sent(f):
         def one(k, _):
-            @pl.when(k != gy)
-            def _():
-                a_copy(f, k).wait_send()
-
-            return 0
-
-        lax.fori_loop(0, GY, one, 0)
+            for xb in range(2):
+                a_copy(f, xb, lax.rem(gy + k, GY)).wait_send()
+            return 0
+
+        lax.fori_loop(1, GY, one, 0)
 
     def all_b_sent(f):
         def one(ky, _):
@@ -486,13 +496,11 @@
 
     def all_ba_sent(step):
         def one(k, _):
-            @pl.when(k != gy)
-            def _():
-                ba_copy(step, k).wait_send()
-
-            return 0
-
-        lax.fori_loop(0, GY, one, 0)
+            for xb in range(2):
+                ba_copy(step, xb, lax.rem(gy + k, GY)).wait_send()
+            return 0
+
+        lax.fori_loop(1, GY, one, 0)
 
     def all_bb_sent(step):
         for slot in range(3):
@@ -525,11 +533,15 @@
 
     def start():
         copies[0].wait()
-        for copy in copies[3:]:
-            copy.start()
-        pad_cells(0)
+        pad_cells(0, 0)
         copies[1].wait()
         copies[2].wait()
+
+    def start_rest():
+        copies[12].wait()
+        for n in range(3, 12):
+            copies[n].start()
+        pad_cells(0, 1)
 
     def unpack_weights():
         def one(i, _):
@@ -548,11 +560,23 @@
         lax.fori_loop(0, C, one, 0)
 
     def meet():
-        pl.semaphore_wait(barrier, GX * GY - 1)
+        pl.semaphore_wait(barrier, GX + GY - 2)
+
+        def one(d, _):
+            pl.semaphore_signal(
+                complete, inc=1, device_id=(lax.rem(gx + d, GX), gy), device_id_type=MESH
+            )
+            return 0
+
+        lax.fori_loop(1, GX, one, 0)
+
+    def meet_all():
+        pl.semaphore_wait(complete, GX - 1)
 
     def load_second():
         copies[4].wait()
-        pad_cells(1)
+        pad_cells(1, 0)
+        pad_cells(1, 1)
 
     def loaded(*numbers):
         for n in numbers:
@@ -569,6 +593,7 @@
         (deep_half, 0, 0, 0),
         (meet,),
         (send_a_half, 0, 0),
+        (start_rest,),
         (deep_half, 0, 0, 1),
         (send_a_half, 0, 1),
         (load_second,),
@@ -577,19 +602,21 @@
         (loaded, 6),
         (unpack_weights,),
         (wait_a, 0),
+        (loaded, 3),
+        (meet_all,),
+        (columns, 0),
         (send_a_half, 1, 0),
-        (send_a_half, 1, 1),
-        (loaded, 3),
-        (columns, 0),
         (loaded, 5, 7),
         (wait_b, 0),
         (rows_forward, 0),
         (mix_and_return, 0, 0, None),
+        (send_a_half, 1, 1),
         (loaded, 8),
         (wait_bb, 0),
         (columns_inverse, 0),
         (wait_a, 1),
         (columns, 1),
+        (send_ba_half, 0, 1),
         (loaded, 9, 10, 11),
         (deep_inverse, 0, 0),
         (pointwise, 0, 0, False),
@@ -608,6 +635,7 @@
         (mix_and_return, 1, 1, (0, 2)),
         (wait_bb, 1),
         (columns_inverse, 1),
+        (send_ba_half, 1, 1),
         (deep_inverse, 1, 0),
         (pointwise, 1, 0, True),
         (deep_half, 3, 1, 0),
@@ -658,14 +686,14 @@
     ]
     scratch += [vmem(table.shape, BF) for table in tables]
     scratch += [
-        vmem((4, GY, 2, 2, 64, 128), BF),
-        vmem((4, GY, 2, 2, 64, 128), BF),
+        vmem((4, 2, GY, 2, 64, 128), BF),
+        vmem((4, 2, GY, 2, 64, 128), BF),
         vmem((4, KY, 16, 128), BF),
         vmem((4, 3, 2, GX, 16, 128), BF),
         vmem((2, 3, 16, 16, 128), BF),
         vmem((2, KY, 16, 128), BF),
-        vmem((2, GY, 2, 2, 64, 128), BF),
-        vmem((2, GY, 2, 2, 64, 128), BF),
+        vmem((2, 2, GY, 2, 64, 128), BF),
+        vmem((2, 2, GY, 2, 64, 128), BF),
         vmem((3, 64, 128), F32),
         vmem((4, 2, C, 432), F32),
         vmem((3, 64, 128), F32),
@@ -673,8 +701,9 @@
         vmem((256, 1024), BF),
         vmem((C, 4, 128, 128), BF),
         vmem((C * 16, C * 16), BF),
-        dma((12,)),
+        dma((13,)),
         dma((2,)),
+        pltpu.SemaphoreType.REGULAR,
         dma((4,)),
         dma((4,)),
         dma((4,)),

time: 187 us -> 156 us (0.83)
  Pallas kernels: 181 us -> 150 us
    pallas_call x1, Pallas kernels: 181 us -> 150 us  [shards(): pl.pallas_call(kernel, out_shape=(jax.ShapeDtypeStruct((C, 15, 32, 128),...]
where the time goes in v4:
time: 156 us
  Pallas kernels  150 us (96%)
  local copies, waits for them, and re-layouts  4.84 us (3%)
    pallas_call x1, Pallas kernels, shards(): pl.pallas_call(kernel, out_shape=(jax.ShapeDtypeStruct((C, 15, 32, 128),...  150 us
    unnamed x4, local copies, waits for them, and re-layouts  4.84 us

profile of v4, /device:TPU:1, one launch (start us, length us, event | category | flops | bytes accessed | tf_op | source)
XLA Modules:
  0.0 155.8 jit_solution(8375899039128059290)
XLA Ops:
  0.6 150.3 %shard_map.140 = (bf16[20,15,32,128]{3,2,1,0:T(8,128)(2,1)}, f32[20,20,2,432]{3,2,1,0:T(2,128)}) custom-call(bf16[2,20,15,32,128]{4,3,2,1,0:T(8,128)(2,1)} %bitcast.5, bf16[2,20,15,32,128]{4,3,2,1,0:T(8,128)(2,1)} %bitcast.6, bf16[20,20]{1,0:T(8,128)(2,1)} %w_ref.1, f32[20]{0:T(128)} %bias_ref.1, f32[20,20,2,432]{3,2,1,0:T(2,128)} %bitcast.8, ...), custom_call_target="tpu_custom_call" | custom-call | tf_op jit(solution)/shard_map/pallas_call | solution.py:716
  150.9 0.0 copy-start
  150.9 3.7 %copy.17 = bf16[20,32,15,128]{3,1,2,0:T(8,128)(2,1)} copy(bf16[20,32,15,128]{3,1,2,0:T(8,128)(2,1)} %bitcast.7) | data formatting | bytes 4915200
  154.6 0.0 copy-done
  154.6 1.2 copy.18
Async XLA Ops:
  150.9 3.7 %copy-start = (f32[20,20,2,432]{3,2,1,0:T(2,128)S(1)}, f32[20,20,2,432]{3,2,1,0:T(2,128)}, u32[]{:S(2)}) copy-start(f32[20,20,2,432]{3,2,1,0:T(2,128)} %get-tuple-element.5) | copy-start | bytes 4147204

commit v5 on v4

--- a/solution.py
+++ b/solution.py
@@ -123,6 +123,11 @@
     me = gx * GY + gy
     my_half = gy // 8
     my_group = gy % 8
+    homes = [(ky * 8 + my_group) // 3 for ky in range(6)]
+    slots = [lax.rem(ky * 8 + my_group, 3) for ky in range(6)]
+    groups = [lax.rem(gy * 3 + slot, 8) for slot in range(3)]
+    lines = [gx * 6 + (gy * 3 + slot) // 8 for slot in range(3)]
+    own = functools.reduce(jnp.logical_or, [group == my_group for group in groups])
 
     loads = [
         (fields_hbm.at[0, :, :, pl.ds(0, 16)], fields.at[0, :, pl.ds(0, 15), pl.ds(0, 16)]),
@@ -220,20 +225,37 @@
     def wait_all(ref, sem):
         pltpu.make_async_copy(ref, ref, sem).wait()
 
-    def b_target(ky):
-        group = lax.rem(ky, 6) * 8 + my_group
-        return ky // 6, group // 3, lax.rem(group, 3)
-
-    def b_copy(f, ky):
-        other_x, other_y, slot = b_target(ky)
+    def b_copy(f, other_x, ky):
         return pltpu.make_async_remote_copy(
-            src_ref=send_b.at[f, ky],
-            dst_ref=recv_b.at[f, slot, my_half, gx],
+            src_ref=send_b.at[f, other_x * 6 + ky],
+            dst_ref=recv_b.at[f, slots[ky], my_half, gx],
             send_sem=b_send.at[f],
             recv_sem=b_recv.at[f],
-            device_id=(other_x, other_y),
+            device_id=(other_x, homes[ky]),
             device_id_type=MESH,
         )
+
+    def send_b_all(f):
+        def one(d, _):
+            other_x = lax.rem(gx + d, GX)
+            for ky in range(6):
+                b_copy(f, other_x, ky).start()
+            return 0
+
+        lax.fori_loop(1, GX, one, 0)
+        for ky in range(6):
+
+            @pl.when(homes[ky] != gy)
+            def _():
+                b_copy(f, gx, ky).start()
+
+            @pl.when(homes[ky] == gy)
+            def _():
+                pltpu.make_async_copy(
+                    send_b.at[f, gx * 6 + ky],
+                    recv_b.at[f, slots[ky], my_half, gx],
+                    b_recv.at[f],
+                ).start()
 
     def columns(f):
         data = jnp.concatenate(
@@ -252,25 +274,7 @@
             send_b[f, pl.ds(part * 24, 24)] = jnp.concatenate(
                 [real.reshape(24, 8, 128), imag.reshape(24, 8, 128)], axis=1
             ).astype(BF)
-
-            def one(k, _):
-                ky = part * 24 + lax.rem(gx * 6 + gy + k, 24)
-                other_x, other_y, slot = b_target(ky)
-                mine = jnp.logical_and(other_x == gx, other_y == gy)
-
-                @pl.when(mine)
-                def _():
-                    pltpu.make_async_copy(
-                        send_b.at[f, ky], recv_b.at[f, slot, my_half, gx], b_recv.at[f]
-                    ).start()
-
-                @pl.when(jnp.logical_not(mine))
-                def _():
-                    b_copy(f, ky).start()
-
-                return 0
-
-            lax.fori_loop(0, 24, one, 0)
+        send_b_all(f)
 
     def rows_forward(f):
         pieces = []
@@ -311,16 +315,37 @@
         zero = jnp.zeros((C, 432), F32)
         return lax.fori_loop(0, C, one, (zero, zero))
 
-    def bb_copy(step, slot, n):
-        group = gy * 3 + slot
+    def bb_copy(step, slot, other_x, xh):
         return pltpu.make_async_remote_copy(
-            src_ref=back_b.at[step, slot, n],
-            dst_ref=got_b.at[step, gx * 6 + group // 8],
+            src_ref=back_b.at[step, slot, xh * 8 + other_x],
+            dst_ref=got_b.at[step, lines[slot]],
             send_sem=bb_send.at[step],
             recv_sem=bb_recv.at[step],
-            device_id=(lax.rem(n, 8), (n // 8) * 8 + lax.rem(group, 8)),
+            device_id=(other_x, xh * 8 + groups[slot]),
             device_id_type=MESH,
         )
+
+    def send_bb_slot(step, slot):
+        def one(d, _):
+            other_x = lax.rem(gx + d, GX)
+            for xh in range(2):
+                bb_copy(step, slot, other_x, xh).start()
+            return 0
+
+        lax.fori_loop(1, GX, one, 0)
+        for xh in range(2):
+
+            @pl.when(xh * 8 + groups[slot] != gy)
+            def _():
+                bb_copy(step, slot, gx, xh).start()
+
+            @pl.when(xh * 8 + groups[slot] == gy)
+            def _():
+                pltpu.make_async_copy(
+                    back_b.at[step, slot, xh * 8 + gx],
+                    got_b.at[step, lines[slot]],
+                    bb_recv.at[step],
+                ).start()
 
     def rows_inverse(step, mixed):
         re, im = mixed
@@ -345,29 +370,7 @@
             high, low = both(high), both(low)
             out = dot_nt(row_back[0], high) + (dot_nt(row_back[0], low) + dot_nt(row_back[1], high))
             back_b[step, slot] = (out * INVERSE_TOTAL).astype(BF).reshape(16, 16, 128)
-            group = gy * 3 + slot
-
-            def one(k, _):
-                n = lax.rem(gx + gy + k, 16)
-                mine = jnp.logical_and(
-                    lax.rem(n, 8) == gx, (n // 8) * 8 + lax.rem(group, 8) == gy
-                )
-
-                @pl.when(mine)
-                def _():
-                    pltpu.make_async_copy(
-                        back_b.at[step, slot, n],
-                        got_b.at[step, gx * 6 + group // 8],
-                        bb_recv.at[step],
-                    ).start()
-
-                @pl.when(jnp.logical_not(mine))
-                def _():
-                    bb_copy(step, slot, n).start()
-
-                return 0
-
-            lax.fori_loop(0, 16, one, 0)
+            send_bb_slot(step, slot)
 
     def ba_copy(step, xb, target):
         return pltpu.make_async_remote_copy(
@@ -475,49 +478,25 @@
         lax.fori_loop(0, 8, one, 0)
 
     def all_a_sent(f):
-        def one(k, _):
-            for xb in range(2):
-                a_copy(f, xb, lax.rem(gy + k, GY)).wait_send()
-            return 0
-
-        lax.fori_loop(1, GY, one, 0)
+        for xb in range(2):
+            wait_all(send_a.at[f, xb, pl.ds(0, GY - 1)], a_send.at[f])
+
+    def all_ba_sent(step):
+        for xb in range(2):
+            wait_all(back_a.at[step, xb, pl.ds(0, GY - 1)], ba_send.at[step])
+
+    def all_small_sent(sem):
+        wait_all(send_b.at[0, pl.ds(0, KY - 1)], sem)
+
+        @pl.when(jnp.logical_not(own))
+        def _():
+            wait_all(send_b.at[0, KY - 1], sem)
 
     def all_b_sent(f):
-        def one(ky, _):
-            other_x, other_y, slot = b_target(ky)
-
-            @pl.when(jnp.logical_not(jnp.logical_and(other_x == gx, other_y == gy)))
-            def _():
-                b_copy(f, ky).wait_send()
-
-            return 0
-
-        lax.fori_loop(0, KY, one, 0)
-
-    def all_ba_sent(step):
-        def one(k, _):
-            for xb in range(2):
-                ba_copy(step, xb, lax.rem(gy + k, GY)).wait_send()
-            return 0
-
-        lax.fori_loop(1, GY, one, 0)
+        all_small_sent(b_send.at[f])
 
     def all_bb_sent(step):
-        for slot in range(3):
-            group = gy * 3 + slot
-
-            def one(n, _):
-                mine = jnp.logical_and(
-                    lax.rem(n, 8) == gx, (n // 8) * 8 + lax.rem(group, 8) == gy
-                )
-
-                @pl.when(jnp.logical_not(mine))
-                def _():
-                    bb_copy(step, slot, n).wait_send()
-
-                return 0
-
-            lax.fori_loop(0, 16, one, 0)
+        all_small_sent(bb_send.at[step])
 
     def mix_and_return(step, f, update):
         rows_inverse(step, mix(f, update))

time: 156 us -> 146 us (0.936)
  Pallas kernels: 150 us -> 140 us
    pallas_call x1, Pallas kernels: 150 us -> 140 us  [shards(): pl.pallas_call(kernel, out_shape=(jax.ShapeDtypeStruct((C, 15, 32, 128),...]
where the time goes in v5:
time: 146 us
  Pallas kernels  140 us (96%)
  local copies, waits for them, and re-layouts  4.84 us (3%)
    pallas_call x1, Pallas kernels, shards(): pl.pallas_call(kernel, out_shape=(jax.ShapeDtypeStruct((C, 15, 32, 128),...  140 us
    unnamed x4, local copies, waits for them, and re-layouts  4.84 us

profile of v5, /device:TPU:1, one launch (start us, length us, event | category | flops | bytes accessed | tf_op | source)
XLA Modules:
  0.0 145.7 jit_solution(6331735350879119391)
XLA Ops:
  0.6 140.2 %shard_map.140 = (bf16[20,15,32,128]{3,2,1,0:T(8,128)(2,1)}, f32[20,20,2,432]{3,2,1,0:T(2,128)}) custom-call(bf16[2,20,15,32,128]{4,3,2,1,0:T(8,128)(2,1)} %bitcast.5, bf16[2,20,15,32,128]{4,3,2,1,0:T(8,128)(2,1)} %bitcast.6, bf16[20,20]{1,0:T(8,128)(2,1)} %w_ref.1, f32[20]{0:T(128)} %bias_ref.1, f32[20,20,2,432]{3,2,1,0:T(2,128)} %bitcast.8, ...), custom_call_target="tpu_custom_call" | custom-call | tf_op jit(solution)/shard_map/pallas_call | solution.py:695
  140.9 0.0 copy-start
  140.9 3.7 %copy.17 = bf16[20,32,15,128]{3,1,2,0:T(8,128)(2,1)} copy(bf16[20,32,15,128]{3,1,2,0:T(8,128)(2,1)} %bitcast.7) | data formatting | bytes 4915200
  144.5 0.0 copy-done
  144.5 1.2 copy.18
Async XLA Ops:
  140.9 3.7 %copy-start = (f32[20,20,2,432]{3,2,1,0:T(2,128)S(1)}, f32[20,20,2,432]{3,2,1,0:T(2,128)}, u32[]{:S(2)}) copy-start(f32[20,20,2,432]{3,2,1,0:T(2,128)} %get-tuple-element.5) | copy-start | bytes 4147204

commit v6 on v5

--- a/solution.py
+++ b/solution.py
@@ -114,7 +114,7 @@
     fields, cots, cells, packed, weights, act,
     deep0, deep1, column, row, row_back, column_back, rise0, rise1,
     send_a, recv_a, send_b, recv_b, back_b, got_b, back_a, got_a,
-    xs, spectra, xi, turned, lifted, branch, kron,
+    xs, spectra, xi, turned, lifted, branch, pre, kron,
     load_sems, out_sems, complete,
     a_send, a_recv, b_send, b_recv, bb_send, bb_recv, ba_send, ba_recv,
 ):
@@ -127,6 +127,13 @@
     slots = [lax.rem(ky * 8 + my_group, 3) for ky in range(6)]
     groups = [lax.rem(gy * 3 + slot, 8) for slot in range(3)]
     lines = [gx * 6 + (gy * 3 + slot) // 8 for slot in range(3)]
+    mates = [
+        lax.rem(gy // 4 + dy, 4) * 4 + lax.rem(gy + dx, 4)
+        for dy, dx in [
+            (2, 2), (0, 2), (2, 0), (1, 2), (2, 1), (3, 2), (2, 3), (1, 1),
+            (3, 3), (1, 3), (3, 1), (0, 1), (1, 0), (0, 3), (3, 0),
+        ]
+    ]
     own = functools.reduce(jnp.logical_or, [group == my_group for group in groups])
 
     loads = [
@@ -215,11 +222,8 @@
         )
 
     def send_a_half(f, xb):
-        def one(k, _):
-            a_copy(f, xb, lax.rem(gy + k, GY)).start()
-            return 0
-
-        lax.fori_loop(1, GY, one, 0)
+        for mate in mates:
+            a_copy(f, xb, mate).start()
         pltpu.make_async_copy(send_a.at[f, xb, gy], recv_a.at[f, xb, gy], a_recv.at[f]).start()
 
     def wait_all(ref, sem):
@@ -394,11 +398,11 @@
             ba_copy(step, xb, target).start()
 
     def send_ba_half(step, xb):
-        def one(k, _):
-            send_ba(step, xb, lax.rem(gy + 1 + k, GY))
-            return 0
-
-        lax.fori_loop(0, GY, one, 0)
+        for mate in mates:
+            ba_copy(step, xb, mate).start()
+        pltpu.make_async_copy(
+            back_a.at[step, xb, gy], got_a.at[step, xb, gy], ba_recv.at[step, xb]
+        ).start()
 
     def columns_inverse(step):
         data = got_b[step].astype(F32)
@@ -442,40 +446,50 @@
         for k in range(2):
             save(dot_nn(lifted[:, 768:1024], rise1[k]), 16 + 2 * k)
 
+    def channel_map(step):
+        for part in range(2):
+
+            def one(k, _):
+                rows = pl.ds(k * 16, 16)
+                data = jnp.concatenate(
+                    [
+                        jnp.concatenate(
+                            [cells[step, c, part * 2 + xh, rows] for c in range(C)], axis=0
+                        )
+                        for xh in range(2)
+                    ],
+                    axis=1,
+                )
+                out = dot_nn(kron[...], data)
+                for o in range(C):
+                    for xh in range(2):
+                        pre[o, part * 2 + xh, rows] = (
+                            out[o * 16 : o * 16 + 16, xh * 128 : xh * 128 + 128] + bias_ref[o]
+                        )
+                return 0
+
+            lax.fori_loop(0, 8, one, 0)
+
     def pointwise(step, part, last):
-        def one(k, _):
-            rows = pl.ds(k * 16, 16)
-            data = jnp.concatenate(
-                [
-                    jnp.concatenate([cells[step, c, part * 2 + xh, rows] for c in range(C)], axis=0)
-                    for xh in range(2)
-                ],
-                axis=1,
-            )
-            pre = dot_nn(kron[...], data)
-            for o in range(C):
-                cot = cots[step, o, pl.ds(2 * k, 2), part * 16 : part * 16 + 16].astype(F32)
-                cot = cot.reshape(2, 2, 8, 128)
-                outs = []
-                for xh in range(2):
-                    v = pre[o * 16 : o * 16 + 16, xh * 128 : xh * 128 + 128]
-                    v = v + (branch[o, part * 2 + xh, rows].astype(F32) + bias_ref[o])
-                    square = v * v
-                    half = 0.5 + 0.5 * jnp.tanh(v * (GELU_K + (GELU_K * GELU_C) * square))
-                    slope = half + (half * (1.0 - half)) * (
-                        v * (2.0 * GELU_K + (6.0 * GELU_K * GELU_C) * square)
-                    )
-                    cells[step, o, part * 2 + xh, rows] = (
-                        cot[:, xh].reshape(16, 128) * slope
-                    ).astype(BF)
-                    outs.append((v * half).reshape(2, 8, 128))
-                if last:
-                    act[o, pl.ds(2 * k, 2), part * 16 : part * 16 + 16] = jnp.concatenate(
-                        outs, axis=1
-                    ).astype(BF)
-            return 0
-
-        lax.fori_loop(0, 8, one, 0)
+        def one(o, _):
+            cot = cots[step, o, :, part * 16 : part * 16 + 16].astype(F32)
+            cot = cot.reshape(16, 2, 8, 128)
+            outs = []
+            for xh in range(2):
+                block = part * 2 + xh
+                v = pre[o, block] + branch[o, block].astype(F32)
+                square = v * v
+                half = 0.5 + 0.5 * jnp.tanh(v * (GELU_K + (GELU_K * GELU_C) * square))
+                slope = half + (half * (1.0 - half)) * (
+                    v * (2.0 * GELU_K + (6.0 * GELU_K * GELU_C) * square)
+                )
+                cells[step, o, block] = (cot[:, xh].reshape(128, 128) * slope).astype(BF)
+                outs.append((v * half).reshape(16, 8, 128))
+            if last:
+                act[o, :, part * 16 : part * 16 + 16] = jnp.concatenate(outs, axis=1).astype(BF)
+            return 0
+
+        lax.fori_loop(0, C, one, 0)
 
     def all_a_sent(f):
         for xb in range(2):
@@ -580,6 +594,7 @@
         (deep_half, 1, 1, 1),
         (loaded, 6),
         (unpack_weights,),
+        (channel_map, 0),
         (wait_a, 0),
         (loaded, 3),
         (meet_all,),
@@ -605,6 +620,7 @@
         (pointwise, 0, 1, False),
         (deep_half, 2, 0, 1),
         (send_a_half, 2, 1),
+        (channel_map, 1),
         (wait_b, 1),
         (rows_forward, 1),
         (wait_a, 2),
@@ -679,6 +695,7 @@
         vmem((256, 768), BF),
         vmem((256, 1024), BF),
         vmem((C, 4, 128, 128), BF),
+        vmem((C, 4, 128, 128), F32),
         vmem((C * 16, C * 16), BF),
         dma((13,)),
         dma((2,)),

time: 146 us -> 140 us (0.959)
  Pallas kernels: 140 us -> 134 us
    pallas_call x1, Pallas kernels: 140 us -> 134 us  [shards(): pl.pallas_call(kernel, out_shape=(jax.ShapeDtypeStruct((C, 15, 32, 128),...]
where the time goes in v6:
time: 140 us
  Pallas kernels  134 us (96%)
  local copies, waits for them, and re-layouts  4.84 us (3%)
    pallas_call x1, Pallas kernels, shards(): pl.pallas_call(kernel, out_shape=(jax.ShapeDtypeStruct((C, 15, 32, 128),...  134 us
    unnamed x4, local copies, waits for them, and re-layouts  4.84 us

profile of v6, /device:TPU:1, one launch (start us, length us, event | category | flops | bytes accessed | tf_op | source)
XLA Modules:
  0.0 139.8 jit_solution(11305177489517616591)
XLA Ops:
  0.6 134.3 %shard_map.140 = (bf16[20,15,32,128]{3,2,1,0:T(8,128)(2,1)}, f32[20,20,2,432]{3,2,1,0:T(2,128)}) custom-call(bf16[2,20,15,32,128]{4,3,2,1,0:T(8,128)(2,1)} %bitcast.5, bf16[2,20,15,32,128]{4,3,2,1,0:T(8,128)(2,1)} %bitcast.6, bf16[20,20]{1,0:T(8,128)(2,1)} %w_ref.1, f32[20]{0:T(128)} %bias_ref.1, f32[20,20,2,432]{3,2,1,0:T(2,128)} %bitcast.8, ...), custom_call_target="tpu_custom_call" | custom-call | tf_op jit(solution)/shard_map/pallas_call | solution.py:712
  135.0 0.0 copy-start
  135.0 3.7 %copy.17 = bf16[20,32,15,128]{3,1,2,0:T(8,128)(2,1)} copy(bf16[20,32,15,128]{3,1,2,0:T(8,128)(2,1)} %bitcast.7) | data formatting | bytes 4915200
  138.7 0.0 copy-done
  138.7 1.2 copy.18
Async XLA Ops:
  135.0 3.7 %copy-start = (f32[20,20,2,432]{3,2,1,0:T(2,128)S(1)}, f32[20,20,2,432]{3,2,1,0:T(2,128)}, u32[]{:S(2)}) copy-start(f32[20,20,2,432]{3,2,1,0:T(2,128)} %get-tuple-element.5) | copy-start | bytes 4147204

commit v7 on v6

--- a/solution.py
+++ b/solution.py
@@ -134,6 +134,7 @@
             (3, 3), (1, 3), (3, 1), (0, 1), (1, 0), (0, 3), (3, 0),
         ]
     ]
+    planes = [lax.rem(gx + d, GX) for d in (4, 5, 3, 2, 6, 7, 1)]
     own = functools.reduce(jnp.logical_or, [group == my_group for group in groups])
 
     loads = [
@@ -240,13 +241,9 @@
         )
 
     def send_b_all(f):
-        def one(d, _):
-            other_x = lax.rem(gx + d, GX)
+        for other_x in planes:
             for ky in range(6):
                 b_copy(f, other_x, ky).start()
-            return 0
-
-        lax.fori_loop(1, GX, one, 0)
         for ky in range(6):
 
             @pl.when(homes[ky] != gy)
@@ -330,13 +327,9 @@
         )
 
     def send_bb_slot(step, slot):
-        def one(d, _):
-            other_x = lax.rem(gx + d, GX)
+        for other_x in planes:
             for xh in range(2):
                 bb_copy(step, slot, other_x, xh).start()
-            return 0
-
-        lax.fori_loop(1, GX, one, 0)
         for xh in range(2):
 
             @pl.when(xh * 8 + groups[slot] != gy)

time: 140 us -> 138 us (0.986)
  Pallas kernels: 134 us -> 132 us
    pallas_call x1, Pallas kernels: 134 us -> 132 us  [shards(): pl.pallas_call(kernel, out_shape=(jax.ShapeDtypeStruct((C, 15, 32, 128),...]
where the time goes in v7:
time: 138 us
  Pallas kernels  132 us (96%)
  local copies, waits for them, and re-layouts  4.84 us (4%)
    pallas_call x1, Pallas kernels, shards(): pl.pallas_call(kernel, out_shape=(jax.ShapeDtypeStruct((C, 15, 32, 128),...  132 us
    unnamed x4, local copies, waits for them, and re-layouts  4.84 us

profile of v7, /device:TPU:1, one launch (start us, length us, event | category | flops | bytes accessed | tf_op | source)
XLA Modules:
  0.0 138.0 jit_solution(9157495675752550742)
XLA Ops:
  0.6 132.5 %shard_map.140 = (bf16[20,15,32,128]{3,2,1,0:T(8,128)(2,1)}, f32[20,20,2,432]{3,2,1,0:T(2,128)}) custom-call(bf16[2,20,15,32,128]{4,3,2,1,0:T(8,128)(2,1)} %bitcast.5, bf16[2,20,15,32,128]{4,3,2,1,0:T(8,128)(2,1)} %bitcast.6, bf16[20,20]{1,0:T(8,128)(2,1)} %w_ref.1, f32[20]{0:T(128)} %bias_ref.1, f32[20,20,2,432]{3,2,1,0:T(2,128)} %bitcast.8, ...), custom_call_target="tpu_custom_call" | custom-call | tf_op jit(solution)/shard_map/pallas_call | solution.py:705
  133.1 0.0 copy-start
  133.1 3.7 %copy.17 = bf16[20,32,15,128]{3,1,2,0:T(8,128)(2,1)} copy(bf16[20,32,15,128]{3,1,2,0:T(8,128)(2,1)} %bitcast.7) | data formatting | bytes 4915200
  136.8 0.0 copy-done
  136.8 1.2 copy.18
Async XLA Ops:
  133.1 3.7 %copy-start = (f32[20,20,2,432]{3,2,1,0:T(2,128)S(1)}, f32[20,20,2,432]{3,2,1,0:T(2,128)}, u32[]{:S(2)}) copy-start(f32[20,20,2,432]{3,2,1,0:T(2,128)} %get-tuple-element.5) | copy-start | bytes 4147204

commit v8 on v7

--- a/solution.py
+++ b/solution.py
@@ -135,6 +135,8 @@
         ]
     ]
     planes = [lax.rem(gx + d, GX) for d in (4, 5, 3, 2, 6, 7, 1)]
+    near_half = gx // 4
+    far_half = 1 - near_half
     own = functools.reduce(jnp.logical_or, [group == my_group for group in groups])
 
     loads = [
@@ -240,10 +242,15 @@
             device_id_type=MESH,
         )
 
-    def send_b_all(f):
-        for other_x in planes:
+    def send_b_far(f):
+        for d in range(4):
             for ky in range(6):
-                b_copy(f, other_x, ky).start()
+                b_copy(f, far_half * 4 + lax.rem(gx + d, 4), ky).start()
+
+    def send_b_near(f):
+        for d in (2, 1, 3):
+            for ky in range(6):
+                b_copy(f, near_half * 4 + lax.rem(gx + d, 4), ky).start()
         for ky in range(6):
 
             @pl.when(homes[ky] != gy)
@@ -268,14 +275,14 @@
             ],
             axis=1,
         )
-        for part in range(2):
+        for part, send in ((far_half, send_b_far), (near_half, send_b_near)):
             out = dot_nt(column[part], data)
             real = out[:192, :128] + out[192:, 128:]
             imag = out[:192, 128:] - out[192:, :128]
             send_b[f, pl.ds(part * 24, 24)] = jnp.concatenate(
                 [real.reshape(24, 8, 128), imag.reshape(24, 8, 128)], axis=1
             ).astype(BF)
-        send_b_all(f)
+            send(f)
 
     def rows_forward(f):
         pieces = []
@@ -304,10 +311,12 @@
                 in_im = spectra[field_f, 1, pl.ds(i, 1), :]
                 w_re = w_re - (in_re * grad_re + in_im * grad_im)
                 w_im = w_im - (in_re * grad_im - in_im * grad_re)
+                if f is None:
+                    packed[i, :, 0, :] = w_re
+                    packed[i, :, 1, :] = w_im
+                    return carry
                 weights[0, i] = w_re
                 weights[1, i] = w_im
-            if f is None:
-                return carry
             re, im = carry
             s_re = spectra[f, 0, pl.ds(i, 1), :]
             s_im = spectra[f, 1, pl.ds(i, 1), :]
@@ -533,14 +542,6 @@
         def one(i, _):
             for part in range(2):
                 weights[part, i] = packed[i, :, part, :]
-            return 0
-
-        lax.fori_loop(0, C, one, 0)
-
-    def pack_weights():
-        def one(i, _):
-            for part in range(2):
-                packed[i, :, part, :] = weights[part, i]
             return 0
 
         lax.fori_loop(0, C, one, 0)
@@ -638,7 +639,6 @@
         (wait_b, 3),
         (rows_forward, 3),
         (mix, None, (1, 3)),
-        (pack_weights,),
     ]
     for stage, *numbers in schedule:
         stage(*numbers)

time: 138 us -> 139 us (level)
  no operation moved by 1% of the time
where the time goes in v8:
time: 139 us; the launch traced here: 138 us
  Pallas kernels  132 us (95%)
  local copies, waits for them, and re-layouts  4.84 us (3%)
    pallas_call x1, Pallas kernels, shards(): pl.pallas_call(kernel, out_shape=(jax.ShapeDtypeStruct((C, 15, 32, 128),...  132 us
    unnamed x4, local copies, waits for them, and re-layouts  4.84 us

profile of v8, /device:TPU:1, one launch (start us, length us, event | category | flops | bytes accessed | tf_op | source)
XLA Modules:
  0.0 137.8 jit_solution(2210708536065310043)
XLA Ops:
  0.6 132.4 %shard_map.140 = (bf16[20,15,32,128]{3,2,1,0:T(8,128)(2,1)}, f32[20,20,2,432]{3,2,1,0:T(2,128)}) custom-call(bf16[2,20,15,32,128]{4,3,2,1,0:T(8,128)(2,1)} %bitcast.5, bf16[2,20,15,32,128]{4,3,2,1,0:T(8,128)(2,1)} %bitcast.6, bf16[20,20]{1,0:T(8,128)(2,1)} %w_ref.1, f32[20]{0:T(128)} %bias_ref.1, f32[20,20,2,432]{3,2,1,0:T(2,128)} %bitcast.8, ...), custom_call_target="tpu_custom_call" | custom-call | tf_op jit(solution)/shard_map/pallas_call | solution.py:705
  133.0 0.0 copy-start
  133.0 3.7 %copy.17 = bf16[20,32,15,128]{3,1,2,0:T(8,128)(2,1)} copy(bf16[20,32,15,128]{3,1,2,0:T(8,128)(2,1)} %bitcast.7) | data formatting | bytes 4915200
  136.7 0.0 copy-done
  136.7 1.2 copy.18
Async XLA Ops:
  133.0 3.7 %copy-start = (f32[20,20,2,432]{3,2,1,0:T(2,128)S(1)}, f32[20,20,2,432]{3,2,1,0:T(2,128)}, u32[]{:S(2)}) copy-start(f32[20,20,2,432]{3,2,1,0:T(2,128)} %get-tuple-element.5) | copy-start | bytes 4147204
